TPU v7x, 32 devices: a whole 2x2x4 slice. The times are simulated.
32 devices in a mesh: dp: 8 (over z, y), seq: 4 (over x, core).
Axes of the slice: x: 2, y: 2, z: 4, core: 2. Of those that a mesh axis runs over, the one named last changes fastest.
Arguments:
- tokens: bfloat16 [4096, 1088], P(('dp', 'seq')), may hold values from -8 to 8
- segment_ids: int32 [8, 512], P('dp'), may hold values from 0 to 3, never falling along the last dimension, each value on 1 to 385 neighbouring positions
- attend_weight: bfloat16 [1088, 3, 1088], P('seq', None, 'dp'), may hold values from -2 to 2
- output_weight: bfloat16 [1088, 1088], P('seq', 'dp'), may hold values from -1 to 1
- expand_weight: bfloat16 [1088, 4352], P('seq', 'dp'), may hold values from -0.1875 to 0.1875
- shrink_weight: bfloat16 [4352, 1088], P('seq', 'dp'), may hold values from -0.09375 to 0.09375
- vectors: bfloat16 [13056], P(('dp', 'seq')), may hold values from -2 to 2
- cotangent: bfloat16 [4096, 1088], P(('dp', 'seq')), may hold values from -6 to 6
Outputs:
- mixed: bfloat16 [4096, 1088], P(('dp', 'seq'))
- tokens_grad: float32 [4096, 1088], P(('dp', 'seq'))
- attend_grad: float32 [1088, 3, 1088], P('seq', None, 'dp')
- output_grad: float32 [1088, 1088], P('seq', 'dp')
- expand_grad: float32 [1088, 4352], P('seq', 'dp')
- shrink_grad: float32 [4352, 1088], P('seq', 'dp')
- vectors_grad: float32 [13056], P(('dp', 'seq'))
Inputs may be any that keep to these rules, and one draw needn't show every extreme that they name: `segment_ids`: in each group the numbers never fall, every number of 0 to 3 occurs, each sequence has 1 to 385 tokens and one has exactly 385.
All inputs are finite; a program needn't handle non-finite values.
Results may differ from a plain program's by a relative error of at most 0.0093.
Values may be sent and summed in bfloat16 or wider, within the bound.
A program may use at most 192 MiB of HBM per device.

v0:
```python
import jax
import jax.numpy as jnp
from jax import lax
from jax.sharding import PartitionSpec as P

D = 1088
H = 17
HD = 64
FF = 4352


EPS = 1e-05


def layer_norm(values):
    centre = values - jnp.mean(values, axis=-1, keepdims=True)
    inverse = lax.rsqrt(jnp.mean(centre * centre, axis=-1, keepdims=True) + EPS)
    return (centre * inverse, inverse)


def norm_back(upstream, normed, inverse, gain):
    scaled = upstream * gain
    return (
        scaled
        - jnp.mean(scaled, axis=-1, keepdims=True)
        - normed * jnp.mean(scaled * normed, axis=-1, keepdims=True)
    ) * inverse


def gelu_parts(pre):
    normal_cdf = 0.5 * (1.0 + lax.erf(pre * 0.7071067811865476))
    density = jnp.exp(-0.5 * pre * pre) * 0.3989422804014327
    return (pre * normal_cdf, normal_cdf + pre * density)


def group_rows(values):
    return lax.all_gather(values, "seq", axis=0, tiled=True)


def whole_columns(values):
    return lax.all_gather(values, "seq", axis=1, tiled=True)


def back_rows(values):
    return lax.all_to_all(values, "seq", split_axis=0, concat_axis=1, tiled=True)


def contract_last(left, right):
    return lax.dot_general(
        left, right, (((1,), (1,)), ((), ())), preferred_element_type=jnp.float32
    )


def body(
    tokens,
    segment_ids,
    attend_weight,
    output_weight,
    expand_weight,
    shrink_weight,
    vectors,
    cotangent,
):
    rows = tokens.shape[0]
    parts = lax.axis_size("seq")
    group = rows * parts
    place = lax.axis_index("seq")
    width_cols = D // parts
    hidden_cols = FF // parts
    segment_all = segment_ids.reshape(-1)
    segment = lax.dynamic_slice_in_dim(segment_all, place * rows, rows, 0)
    vector_flat = lax.all_gather(vectors, ("dp", "seq"), axis=0, tiled=True)
    table = vector_flat[: 8 * D].astype(jnp.float32).reshape(8, D)
    fc_bias = vector_flat[8 * D :].astype(jnp.float32)
    attend_rows, output_rows, expand_rows, shrink_rows = (
        lax.all_gather(attend_weight, "dp", axis=2, tiled=True),
        lax.all_gather(output_weight, "dp", axis=1, tiled=True),
        lax.all_gather(expand_weight, "dp", axis=1, tiled=True),
        lax.all_gather(shrink_weight, "dp", axis=1, tiled=True),
    )
    attend_cols, output_cols, expand_cols, shrink_cols = (
        lax.all_to_all(attend_rows, "seq", split_axis=2, concat_axis=0, tiled=True),
        lax.all_to_all(output_rows[:, None, :], "seq", split_axis=2, concat_axis=0, tiled=True),
        lax.all_to_all(expand_rows[:, None, :], "seq", split_axis=2, concat_axis=0, tiled=True),
        lax.all_to_all(shrink_rows[:, None, :], "seq", split_axis=2, concat_axis=0, tiled=True),
    )
    shrink_cols = shrink_cols.reshape(FF, width_cols)
    output_cols = output_cols.reshape(D, width_cols)
    expand_cols = expand_cols.reshape(D, hidden_cols)
    inputs32 = tokens.astype(jnp.float32)
    normed_one, inverse_one = layer_norm(inputs32)
    hidden_one = (normed_one * table[0] + table[1]).astype(jnp.bfloat16)
    hidden_one_all = group_rows(hidden_one)
    projected = jnp.einsum(
        "gd,dkc->gkc", hidden_one_all, attend_cols, preferred_element_type=jnp.float32
    )
    query_bias = lax.dynamic_slice_in_dim(table[2], place * width_cols, width_cols, 0)
    value_bias = lax.dynamic_slice_in_dim(table[3], place * width_cols, width_cols, 0)
    bias_cols = jnp.stack((query_bias, jnp.zeros_like(query_bias), value_bias))
    triple_cols = (projected + bias_cols[None]).astype(jnp.bfloat16)
    triple_all = lax.all_gather(triple_cols, "seq", axis=2, tiled=True)
    query_all_heads = triple_all[:, 0].reshape(group, H, HD)
    key_heads = triple_all[:, 1].reshape(group, H, HD)
    value_heads = triple_all[:, 2].reshape(group, H, HD)
    query_heads = lax.dynamic_slice_in_dim(query_all_heads, place * rows, rows, 0)
    own_keys = lax.dynamic_slice_in_dim(key_heads, place * rows, rows, 0)
    own_values = lax.dynamic_slice_in_dim(value_heads, place * rows, rows, 0)
    query_pos = place * rows + jnp.arange(rows, dtype=jnp.int32)
    key_pos = jnp.arange(group, dtype=jnp.int32)
    allowed = (key_pos[None, :] <= query_pos[:, None]) & (segment_all[None, :] == segment[:, None])
    scores = (
        jnp.einsum("thd,ghd->htg", query_heads, key_heads, preferred_element_type=jnp.float32)
        * 0.125
    )
    scores = jnp.where(allowed[None], scores, -jnp.inf)
    peak = jnp.max(scores, axis=-1, keepdims=True)
    log_total = peak + jnp.log(jnp.sum(jnp.exp(scores - peak), axis=-1, keepdims=True))
    probs = jnp.exp(scores - log_total)
    probs_low = probs.astype(jnp.bfloat16)
    context = jnp.einsum("htg,ghd->thd", probs_low, value_heads, preferred_element_type=jnp.float32)
    context = context.reshape(rows, D).astype(jnp.bfloat16)
    context_all = group_rows(context)
    attn_cols = jnp.dot(context_all, output_cols, preferred_element_type=jnp.float32)
    residual = inputs32 + back_rows(attn_cols) + table[4]
    normed_two, inverse_two = layer_norm(residual)
    hidden_two = (normed_two * table[5] + table[6]).astype(jnp.bfloat16)
    hidden_two_all = group_rows(hidden_two)
    fc_cols = lax.dynamic_slice_in_dim(fc_bias, place * hidden_cols, hidden_cols, 0)
    pre = jnp.dot(hidden_two_all, expand_cols, preferred_element_type=jnp.float32) + fc_cols
    activated, slope = gelu_parts(pre)
    activated_low = activated.astype(jnp.bfloat16)
    activated_all = whole_columns(activated_low)
    branch = back_rows(jnp.dot(activated_all, shrink_cols, preferred_element_type=jnp.float32))
    mixed = (residual + branch + table[7]).astype(jnp.bfloat16)
    attend_rows, output_rows, expand_rows, shrink_rows = (
        lax.all_gather(attend_weight, "dp", axis=2, tiled=True),
        lax.all_gather(output_weight, "dp", axis=1, tiled=True),
        lax.all_gather(expand_weight, "dp", axis=1, tiled=True),
        lax.all_gather(shrink_weight, "dp", axis=1, tiled=True),
    )
    upstream = cotangent.astype(jnp.float32)
    upstream_all = group_rows(cotangent)
    shrink_grad = jnp.dot(activated_low.T, upstream_all, preferred_element_type=jnp.float32)
    pre_grad = contract_last(upstream_all, shrink_rows) * slope
    pre_low = pre_grad.astype(jnp.bfloat16)
    pre_all = whole_columns(pre_low)
    hidden_two_cols = lax.dynamic_slice_in_dim(hidden_two_all, place * width_cols, width_cols, 1)
    expand_grad = jnp.dot(hidden_two_cols.T, pre_all, preferred_element_type=jnp.float32)
    hidden_two_grad = back_rows(contract_last(pre_all, expand_rows))
    residual_grad = upstream + norm_back(hidden_two_grad, normed_two, inverse_two, table[5])
    residual_low = residual_grad.astype(jnp.bfloat16)
    residual_all = group_rows(residual_low)
    context_cols = lax.dynamic_slice_in_dim(context_all, place * width_cols, width_cols, 1)
    output_grad = jnp.dot(context_cols.T, residual_all, preferred_element_type=jnp.float32)
    grad_cols = contract_last(residual_all, output_rows).astype(jnp.bfloat16)
    grad_all = whole_columns(grad_cols)
    grad_all_heads = grad_all.reshape(group, H, HD)
    grad_heads = lax.dynamic_slice_in_dim(grad_all_heads, place * rows, rows, 0)
    totals_all = lax.all_gather(log_total[:, :, 0], "seq", axis=1, tiled=True)
    row_dots = jnp.einsum(
        "thd,thd->ht", grad_heads, context.reshape(rows, H, HD), preferred_element_type=jnp.float32
    )[:, :, None]
    prob_grad = jnp.einsum(
        "thd,ghd->htg", grad_heads, value_heads, preferred_element_type=jnp.float32
    )
    score_grad = (probs * (prob_grad - row_dots)).astype(jnp.bfloat16)
    query_grad = (
        jnp.einsum("htg,ghd->thd", score_grad, key_heads, preferred_element_type=jnp.float32)
        * 0.125
    )
    query_grad = query_grad.reshape(rows, D)
    all_dots = jnp.einsum(
        "ghd,ghd->hg",
        grad_all_heads,
        context_all.reshape(group, H, HD),
        preferred_element_type=jnp.float32,
    )[:, :, None]
    own_allowed = (query_pos[None, :] <= key_pos[:, None]) & (
        segment_all[:, None] == segment[None, :]
    )
    own_scores = (
        jnp.einsum("ghd,khd->hgk", query_all_heads, own_keys, preferred_element_type=jnp.float32)
        * 0.125
    )
    own_scores = jnp.where(own_allowed[None], own_scores, -jnp.inf)
    own_probs = jnp.exp(own_scores - totals_all[:, :, None])
    own_prob_grad = jnp.einsum(
        "ghd,khd->hgk", grad_all_heads, own_values, preferred_element_type=jnp.float32
    )
    own_score_grad = (own_probs * (own_prob_grad - all_dots)).astype(jnp.bfloat16)
    key_grad = (
        jnp.einsum(
            "hgk,ghd->khd", own_score_grad, query_all_heads, preferred_element_type=jnp.float32
        ).reshape(rows, D)
        * 0.125
    )
    value_grad = jnp.einsum(
        "hgk,ghd->khd",
        own_probs.astype(jnp.bfloat16),
        grad_all_heads,
        preferred_element_type=jnp.float32,
    ).reshape(rows, D)
    joined_low = jnp.concatenate((query_grad, key_grad, value_grad), axis=1).astype(jnp.bfloat16)
    joined_all = group_rows(joined_low).reshape(group, 3, D)
    hidden_one_cols = lax.dynamic_slice_in_dim(hidden_one_all, place * width_cols, width_cols, 1)
    attend_grad = jnp.einsum(
        "gi,gkd->ikd", hidden_one_cols, joined_all, preferred_element_type=jnp.float32
    )
    hidden_one_grad = back_rows(
        jnp.einsum("gkd,ikd->gi", joined_all, attend_rows, preferred_element_type=jnp.float32)
    )
    tokens_grad = residual_grad + norm_back(hidden_one_grad, normed_one, inverse_one, table[0])
    vector_rows = jnp.stack(
        (
            jnp.sum(hidden_one_grad * normed_one, axis=0),
            jnp.sum(hidden_one_grad, axis=0),
            jnp.sum(query_grad, axis=0),
            jnp.sum(value_grad, axis=0),
            jnp.sum(residual_grad, axis=0),
            jnp.sum(hidden_two_grad * normed_two, axis=0),
            jnp.sum(hidden_two_grad, axis=0),
            jnp.sum(upstream, axis=0),
        )
    )
    fc_part = jnp.sum(pre_grad, axis=0)
    fc_full = lax.dynamic_update_slice(
        jnp.zeros((FF,), jnp.float32), fc_part, (place * hidden_cols,)
    )
    vector_grad = jnp.concatenate((vector_rows.reshape(-1), fc_full))
    vector_sum = lax.psum_scatter(vector_grad, ("dp", "seq"), scatter_dimension=0, tiled=True)
    weight_sums = (
        lax.psum_scatter(attend_grad, "dp", scatter_dimension=2, tiled=True),
        lax.psum_scatter(output_grad, "dp", scatter_dimension=1, tiled=True),
        lax.psum_scatter(expand_grad, "dp", scatter_dimension=1, tiled=True),
        lax.psum_scatter(shrink_grad, "dp", scatter_dimension=1, tiled=True),
    )
    return (
        mixed,
        tokens_grad,
        weight_sums[0],
        weight_sums[1],
        weight_sums[2],
        weight_sums[3],
        vector_sum,
    )


def solution(mesh):
    return jax.shard_map(
        body,
        mesh=mesh,
        in_specs=(
            P(("dp", "seq"), None),
            P("dp", None),
            P("seq", None, "dp"),
            P("seq", "dp"),
            P("seq", "dp"),
            P("seq", "dp"),
            P(("dp", "seq")),
            P(("dp", "seq"), None),
        ),
        out_specs=(
            P(("dp", "seq"), None),
            P(("dp", "seq"), None),
            P("seq", None, "dp"),
            P("seq", "dp"),
            P("seq", "dp"),
            P("seq", "dp"),
            P(("dp", "seq")),
        ),
        check_vma=False,
    )
```

profile of v0, /device:TPU:0, one launch (start us, length us, event | category | flops | bytes accessed | tf_op | source)
XLA Modules:
  0.0 1031.0 jit_solution(4517816039620645188)
XLA Ops:
  8.8 42.8 %all-reduce = bf16[13056]{0:T(1024)(128)(2,1)S(1)} all-reduce(bf16[13056]{0:T(1024)(128)(2,1)S(1)} %dynamic-update-slice), channel_id=1, replica_groups=mesh['dp'=8,'seq'=4] {'dp','seq'}, use_global_device_ids=true, to_apply=%add | all-reduce | flops 13056 | bytes 52224
  56.7 10.9 %all-gather.17.cloned.1.call-done = bf16[272,3,1088]{0,2,1:T(8,128)(2,1)} async-done(((bf16[272,3,136]{0,2,1:T(8,128)(2,1)}), bf16[272,3,1088]{0,2,1:T(8,128)(2,1)}) %all-gather.17.cloned.1.call-update) | async-done | bytes 1775632 | tf_op jit(solution)/shard_map/all_gather | solution.py:76
  67.5 10.5 %copy.73 = bf16[272,3,1088]{0,1,2:T(4,128)(2,1)} copy(bf16[272,3,1088]{0,2,1:T(8,128)(2,1)} %all-gather.17.cloned.1.call-done) | data formatting | bytes 3551232 | tf_op jit(solution)/shard_map/all_gather | solution.py:76
  78.1 3.7 all-to-all-start
  82.2 38.6 %all-to-all-done = bf16[272,3,1088]{0,1,2:T(4,128)(2,1)S(1)} async-done(((bf16[272,3,1088]{0,1,2:T(4,128)(2,1)}), bf16[272,3,1088]{0,1,2:T(4,128)(2,1)S(1)}, u32[]{:S(2)}, u32[]{:S(2)}) %all-to-all-start) | async-done | bytes 1775648 | tf_op jit(solution)/shard_map/all_to_all | solution.py:82
  120.8 3.8 copy.122
  124.6 4.1 all_to_all.99
  128.8 3.4 add_convert_fusion
  132.7 28.2 %all-gather.19.cloned.1.call-done = bf16[512,3,1088]{0,2,1:T(8,128)(2,1)} async-done(((bf16[512,3,272]{0,2,1:T(8,128)(2,1)}), bf16[512,3,1088]{0,2,1:T(8,128)(2,1)}) %all-gather.19.cloned.1.call-update) | async-done | bytes 3342352 | tf_op jit(solution)/shard_map/all_gather | solution.py:101
  169.2 32.6 %all_gather.57 = bf16[272,1088]{0,1:T(8,128)(2,1)S(1)} all-gather(bf16[272,136]{0,1:T(8,128)(2,1)S(1)} %copy-done.24), channel_id=1, replica_groups=mesh['dp'=8,'seq'=4] {'dp'}, dimensions={1}, use_global_device_ids=true | all-gather | bytes 665856 | tf_op jit(solution)/shard_map/all_gather | solution.py:77
  202.8 15.9 %copy.125 = bf16[272,1,1088]{0,1,2:T(2,128)(2,1)S(1)} copy(bf16[272,1,1088]{0,2,1:T(8,128)(2,1)S(1)} %bitcast.184) | data formatting | bytes 1183744 | tf_op jit(solution)/shard_map/broadcast_in_dim | solution.py:83
  219.2 7.1 reduce.10
  227.7 12.0 %all_to_all.130 = bf16[4,2,36992]{2,1,0:T(2,128)(2,1)S(1)} all-to-all(bf16[4,2,36992]{2,1,0:T(2,128)(2,1)S(1)} %reshape.317), channel_id=1, replica_groups=mesh['dp'=8,'seq'=4] {'seq'}, dimensions={0} | all-to-all | bytes 1183744 | tf_op jit(solution)/shard_map/all_to_all | solution.py:83
  241.6 3.7 copy.78
  250.1 12.0 %all_to_all.131 = f32[4,128,272]{1,2,0:T(8,128)S(1)} all-to-all(f32[4,128,272]{1,2,0:T(8,128)S(1)} %fusion.109), channel_id=1, replica_groups=mesh['dp'=8,'seq'=4] {'seq'}, dimensions={0} | all-to-all | bytes 1114112 | tf_op jit(solution)/shard_map/all_to_all | solution.py:45
  265.1 2.4 copy.81
  267.5 3.1 reshape.297
  270.6 14.2 %copy.82 = bf16[272,1,4352]{0,1,2:T(2,128)(2,1)} copy(bf16[272,1,4352]{2,0,1:T(8,128)(2,1)} %bitcast.171) | data formatting | bytes 4734976 | tf_op jit(solution)/shard_map/broadcast_in_dim | solution.py:84
  284.8 29.4 %reduce.11 = bf16[4352,272]{1,0:T(8,128)(2,1)} reduce(bf16[4352,1,272]{2,1,0:T(2,128)(2,1)} %bitcast.160, bf16[]{:T(256)} %broadcast.170), dimensions={1}, to_apply=%bitcast.120.reduce_sub_computation | reduce | bytes 4734978
  314.2 7.6 reshape.319
  321.7 3.6 all-to-all-start.3
  325.5 28.4 %all-to-all-done.3 = bf16[4,2,147968]{2,1,0:T(2,128)(2,1)S(1)} async-done(((bf16[4,2,147968]{2,1,0:T(2,128)(2,1)}), bf16[4,2,147968]{2,1,0:T(2,128)(2,1)S(1)}, u32[]{:S(2)}, u32[]{:S(2)}) %all-to-all-start.3) | async-done | bytes 2367520 | tf_op jit(solution)/shard_map/all_to_all | solution.py:84
  353.9 7.5 reshape.320
  361.4 13.9 %copy.83 = bf16[272,1,4352]{2,0,1:T(8,128)(2,1)} copy(bf16[272,1,4352]{0,1,2:T(2,128)(2,1)} %bitcast.159) | data formatting | bytes 4734976 | tf_op jit(solution)/shard_map/all_to_all | solution.py:84
  375.3 5.4 all_to_all.107
  382.4 5.6 multiply_convert_fusion.2
  388.0 6.8 fusion.102
  395.4 16.9 %copy.124 = bf16[1088,1,1088]{0,1,2:T(2,128)(2,1)} copy(bf16[1088,1,1088]{0,2,1:T(8,128)(2,1)S(1)} %bitcast.186) | data formatting | bytes 4734976 | tf_op jit(solution)/shard_map/broadcast_in_dim | solution.py:85
  412.4 15.7 %reduce.12 = bf16[1088,1088]{1,0:T(8,128)(2,1)S(1)} reduce(bf16[1088,1,1088]{2,1,0:T(2,128)(2,1)} %bitcast.161, bf16[]{:T(256)} %broadcast.170), dimensions={1}, to_apply=%bitcast.157.reduce_sub_computation | reduce | bytes 4734978
  428.1 3.9 reshape.321
  432.0 3.6 all-to-all-start.4
  436.3 49.3 %all-to-all-done.4 = bf16[4,2,147968]{2,1,0:T(2,128)(2,1)S(1)} async-done(((bf16[4,2,147968]{2,1,0:T(2,128)(2,1)}), bf16[4,2,147968]{2,1,0:T(2,128)(2,1)S(1)}, u32[]{:S(2)}, u32[]{:S(2)}) %all-to-all-start.4) | async-done | bytes 2367520 | tf_op jit(solution)/shard_map/all_to_all | solution.py:85
  485.6 4.5 reshape.322
  490.1 2.8 copy.116
  493.9 3.0 reshape.300
  496.9 4.4 convolution_bitcast_fusion.1
  502.1 3.5 all-to-all-start.6
  505.6 6.6 copy.109
  512.2 4.5 fusion.110
  516.7 3.6 all-to-all-start.5
  523.3 6.2 all-to-all-done.5
  531.6 17.7 %all-gather.33.cloned.1.call-done = bf16[512,1088]{0,1:T(8,128)(2,1)} async-done(((bf16[128,1088]{0,1:T(8,128)(2,1)}), bf16[512,1088]{0,1:T(8,128)(2,1)}) %all-gather.33.cloned.1.call-update) | async-done | bytes 1114128 | tf_op jit(solution)/shard_map/all_gather | solution.py:37
  549.3 2.5 convolution_convert_fusion
  552.1 5.4 all_gather.66
  557.6 3.0 fusion.72
  560.5 8.6 all-gather.35.cloned.1.call-done
  571.0 2.2 fusion.13
  573.2 5.8 fusion.104
  579.0 6.7 fusion.39
  585.6 5.0 fusion.105
  591.8 7.7 convolution_bitcast_fusion
  601.4 3.9 fusion.111
  608.8 13.2 %all-gather.37.cloned.1.call-done = bf16[512,3264]{0,1:T(8,128)(2,1)} async-done(((bf16[128,3264]{0,1:T(8,128)(2,1)}), bf16[512,3264]{0,1:T(8,128)(2,1)}) %all-gather.37.cloned.1.call-update) | async-done | bytes 3342352 | tf_op jit(solution)/shard_map/all_gather | solution.py:37
  622.0 6.2 fusion.64
  630.1 3.8 copy.90
  634.0 4.9 fusion.33
  638.9 3.6 all-to-all-start.7
  643.2 8.5 all-to-all-done.7
  653.9 43.6 %all-reduce.3 = f32[13056]{0:T(1024)S(1)} all-reduce(f32[13056]{0:T(1024)S(1)} %pad_maximum_fusion.1), channel_id=6, replica_groups=mesh['dp'=8,'seq'=4] {'dp','seq'}, use_global_device_ids=true, to_apply=%region_23.24.clone | all-reduce | flops 13056 | bytes 104448
  698.2 52.0 %reduce-scatter.13.cloned.1.call-done = f32[544,272]{1,0:T(8,128)} async-done(((f32[4352,272]{1,0:T(8,128)}), f32[544,272]{1,0:T(8,128)}) %reduce-scatter.13.cloned.1.call-update) | async-done | bytes 591888
  750.2 2.3 copy.115
  752.5 100.8 %reduce-scatter.17.cloned.1.call-done = f32[1088,136]{0,1:T(8,128)} async-done(((f32[1088,1088]{0,1:T(8,128)}), f32[1088,136]{0,1:T(8,128)}) %reduce-scatter.17.cloned.1.call-update) | async-done | bytes 591888
  853.3 68.1 %reduce-scatter.15.cloned.1.call-done = f32[272,136]{0,1:T(8,128)} async-done(((f32[272,1088]{0,1:T(8,128)}), f32[272,136]{0,1:T(8,128)}) %reduce-scatter.15.cloned.1.call-update) | async-done | bytes 147984
  921.4 102.6 %reduce-scatter.11.cloned.1.call-done = f32[272,3,136]{0,2,1:T(8,128)} async-done(((f32[272,3,1088]{0,2,1:T(8,128)}), f32[272,3,136]{0,2,1:T(8,128)}) %reduce-scatter.11.cloned.1.call-update) | async-done | bytes 443920 | tf_op jit(solution)/shard_map/reduce_scatter | solution.py:232
  (205 shorter events, 52.0 us)
Async XLA Ops:
  7.2 60.4 %all-gather.17.cloned.1.call-start = ((), (), s32[]{:S(2)}) async-start(), calls=%async_computation.13 | async-start | bytes 2820096 | tf_op jit(solution)/shard_map/all_gather | solution.py:76
  7.9 120.9 %all-gather.15.cloned.1.call-start = ((), (), s32[]{:S(2)}) async-start(), calls=%async_computation.12 | async-start | bytes 1392640 | tf_op jit(solution)/shard_map/all_gather | solution.py:37
  52.8 25.3 %copy-start.31 = (f32[128]{0:T(128)}, f32[128]{0:T(128)S(1)}, u32[]{:S(2)}) copy-start(f32[128]{0:T(128)S(1)} %broadcast_multiply_fusion.5) | copy-start | bytes 1540
  53.9 24.1 %copy-start.38 = (f32[128]{0:T(128)}, f32[128]{0:T(128)S(1)}, u32[]{:S(2)}) copy-start(f32[128]{0:T(128)S(1)} %add_rsqrt_fusion.1) | copy-start | bytes 1540
  54.6 381.0 %copy-start.22 = (f32[1088]{0:T(1024)}, f32[1088]{0:T(1024)S(1)}, u32[]{:S(2)}) copy-start(f32[1088]{0:T(1024)S(1)} %get-tuple-element.34) | copy-start | bytes 13060
  78.1 42.7 %all-to-all-start = ((bf16[272,3,1088]{0,1,2:T(4,128)(2,1)}), bf16[272,3,1088]{0,1,2:T(4,128)(2,1)S(1)}, u32[]{:S(2)}, u32[]{:S(2)}) async-start(bf16[272,3,1088]{0,1,2:T(4,128)(2,1)} %copy.73), calls=%async_computation | async-start | bytes 6684672 | tf_op jit(solution)/shard_map/all_to_all | solution.py:82
  81.8 79.1 %all-gather.19.cloned.1.call-start = ((), (), s32[]{:S(2)}) async-start(), calls=%async_computation.14 | async-start | bytes 4177920 | tf_op jit(solution)/shard_map/all_gather | solution.py:101
  128.8 3.8 copy-start.33
  132.3 115.5 %all-gather.21.cloned.1.call-start = ((), (), s32[]{:S(2)}) async-start(), calls=%async_computation.15 | async-start | bytes 1392640 | tf_op jit(solution)/shard_map/all_gather | solution.py:37
  132.6 30.5 %copy-start.42 = (s32[128]{0:T(128)}, s32[128]{0:T(128)S(1)}, u32[]{:S(2)}) copy-start(s32[128]{0:T(128)S(1)} %iota_add_fusion) | copy-start | bytes 1540
  132.6 30.5 %copy-start.44 = (s32[128]{0:T(128)}, s32[128]{0:T(128)S(1)}, u32[]{:S(2)}) copy-start(s32[128]{0:T(128)S(1)} %fusion.89) | copy-start | bytes 1540
  163.1 2.7 copy-start.16
  164.5 2.1 copy-start.1
  165.8 2.8 copy-start.25
  166.6 2.6 copy-start.24
  168.6 96.5 %all-gather.39.cloned.1.call-start = ((), (), s32[]{:S(2)}) async-start(), calls=%async_computation.25 | async-start | bytes 3133440 | tf_op jit(solution)/shard_map/all_gather | solution.py:78
  169.2 213.2 %all-gather.23.cloned.1.call-start = ((), (), s32[]{:S(2)}) async-start(), calls=%async_computation.16 | async-start | bytes 1392640 | tf_op jit(solution)/shard_map/all_gather | solution.py:37
  249.5 12.6 %copy-start.2 = (bf16[128,1088]{0,1:T(8,128)(2,1)S(1)}, bf16[128,1088]{0,1:T(8,128)(2,1)}, u32[]{:S(2)}) copy-start(bf16[128,1088]{0,1:T(8,128)(2,1)} %param.8) | copy-start | bytes 835588
  262.3 5.2 copy-start.36
  262.5 5.0 copy-start.40
  263.6 124.5 %all-gather.29.cloned.1.call-start = ((), (), s32[]{:S(2)}) async-start(), calls=%async_computation.19 | async-start | bytes 1392640 | tf_op jit(solution)/shard_map/all_gather | solution.py:37
  264.3 123.7 %all-gather.27.cloned.1.call-start = ((), (), s32[]{:S(2)}) async-start(), calls=%async_computation.18 | async-start | bytes 2820096 | tf_op jit(solution)/shard_map/all_gather | solution.py:79
  321.7 32.2 %all-to-all-start.3 = ((bf16[4,2,147968]{2,1,0:T(2,128)(2,1)}), bf16[4,2,147968]{2,1,0:T(2,128)(2,1)S(1)}, u32[]{:S(2)}, u32[]{:S(2)}) async-start(bf16[4,2,147968]{2,1,0:T(2,128)(2,1)} %reshape.319), calls=%async_computation.3 | async-start | bytes 4734976 | tf_op jit(solution)/shard_map/all_to_all | solution.py:84
  325.3 171.5 %all-gather.31.cloned.1.call-start = ((), (), s32[]{:S(2)}) async-start(), calls=%async_computation.20 | async-start | bytes 5570560 | tf_op jit(solution)/shard_map/all_gather | solution.py:41
  388.0 7.4 copy-start.12
  394.8 110.7 %all-gather.25.cloned.1.call-start = ((), (), s32[]{:S(2)}) async-start(), calls=%async_computation.17 | async-start | bytes 5570560 | tf_op jit(solution)/shard_map/all_gather | solution.py:41
  432.0 53.6 %all-to-all-start.4 = ((bf16[4,2,147968]{2,1,0:T(2,128)(2,1)}), bf16[4,2,147968]{2,1,0:T(2,128)(2,1)S(1)}, u32[]{:S(2)}, u32[]{:S(2)}) async-start(bf16[4,2,147968]{2,1,0:T(2,128)(2,1)} %reshape.321), calls=%async_computation.4 | async-start | bytes 4734976 | tf_op jit(solution)/shard_map/all_to_all | solution.py:85
  502.1 14.7 %all-to-all-start.6 = ((f32[4,128,272]{1,2,0:T(8,128)}), f32[4,128,272]{1,2,0:T(8,128)S(1)}, u32[]{:S(2)}, u32[]{:S(2)}) async-start(f32[4,128,272]{1,2,0:T(8,128)} %bitcast.156), calls=%async_computation.6 | async-start | bytes 1114112 | tf_op jit(solution)/shard_map/all_to_all | solution.py:45
  505.6 6.7 copy-start.13
  516.7 12.8 %copy-start.18 = (bf16[128,1088]{0,1:T(8,128)(2,1)S(1)}, bf16[128,1088]{0,1:T(8,128)(2,1)}, u32[]{:S(2)}) copy-start(bf16[128,1088]{0,1:T(8,128)(2,1)} %param.15) | copy-start | bytes 835588
  516.7 12.8 %copy-start.23 = (f32[1088]{0:T(1024)S(1)}, f32[1088]{0:T(1024)}, u32[]{:S(2)}) copy-start(f32[1088]{0:T(1024)} %copy-done.22) | copy-start | bytes 13060
  516.7 12.8 %copy-start.27 = (f32[1088]{0:T(1024)S(1)}, f32[1088]{0:T(1024)}, u32[]{:S(2)}) copy-start(f32[1088]{0:T(1024)} %get-tuple-element.32) | copy-start | bytes 13060
  516.7 12.8 %copy-start.37 = (f32[128]{0:T(128)S(1)}, f32[128]{0:T(128)}, u32[]{:S(2)}) copy-start(f32[128]{0:T(128)} %copy-done.36) | copy-start | bytes 1540
  516.7 12.8 %copy-start.41 = (f32[128]{0:T(128)S(1)}, f32[128]{0:T(128)}, u32[]{:S(2)}) copy-start(f32[128]{0:T(128)} %copy-done.40) | copy-start | bytes 1540
  516.7 12.8 %all-to-all-start.5 = ((f32[4,128,272]{1,2,0:T(8,128)}), f32[4,128,272]{1,2,0:T(8,128)S(1)}, u32[]{:S(2)}, u32[]{:S(2)}) async-start(f32[4,128,272]{1,2,0:T(8,128)} %fusion.110), calls=%async_computation.5 | async-start | bytes 1114112 | tf_op jit(solution)/shard_map/all_to_all | solution.py:45
  520.4 29.0 %all-gather.33.cloned.1.call-start = ((), (), s32[]{:S(2)}) async-start(), calls=%async_computation.21 | async-start | bytes 1392640 | tf_op jit(solution)/shard_map/all_gather | solution.py:37
  522.1 27.2 %copy-start.11 = (bf16[272,1088]{0,1:T(8,128)(2,1)S(1)}, bf16[272,1088]{0,1:T(8,128)(2,1)}, u32[]{:S(2)}) copy-start(bf16[272,1088]{0,1:T(8,128)(2,1)} %copy-done.10) | copy-start | bytes 1775620
  531.5 20.4 %copy-start.34 = (s32[1,512]{1,0:T(1,128)S(1)}, s32[1,512]{1,0:T(1,128)}, u32[]{:S(2)}) copy-start(s32[1,512]{1,0:T(1,128)} %param.9) | copy-start | bytes 6148
  531.5 20.4 %copy-start.43 = (s32[128]{0:T(128)S(1)}, s32[128]{0:T(128)}, u32[]{:S(2)}) copy-start(s32[128]{0:T(128)} %copy-done.42) | copy-start | bytes 1540
  531.5 20.4 %copy-start.45 = (s32[128]{0:T(128)S(1)}, s32[128]{0:T(128)}, u32[]{:S(2)}) copy-start(s32[128]{0:T(128)} %copy-done.44) | copy-start | bytes 1540
  531.5 20.6 %copy-start.26 = (f32[17,128]{1,0:T(8,128)S(1)}, f32[17,128]{1,0:T(8,128)}, u32[]{:S(2)}) copy-start(f32[17,128]{1,0:T(8,128)} %copy-done.25) | copy-start | bytes 26116
  531.5 26.0 %copy-start.5 = (bf16[512,1,1088]{0,2,1:T(8,128)(2,1)S(1)}, bf16[512,1,1088]{0,2,1:T(8,128)(2,1)}, u32[]{:S(2)}) copy-start(bf16[512,1,1088]{0,2,1:T(8,128)(2,1)} %copy-done.4) | copy-start | bytes 3342340
  531.5 26.0 %copy-start.8 = (bf16[512,1,1088]{0,2,1:T(8,128)(2,1)S(1)}, bf16[512,1,1088]{0,2,1:T(8,128)(2,1)}, u32[]{:S(2)}) copy-start(bf16[512,1,1088]{0,2,1:T(8,128)(2,1)} %copy-done.7) | copy-start | bytes 3342340
  531.6 37.6 %all-gather.35.cloned.1.call-start = ((), (), s32[]{:S(2)}) async-start(), calls=%async_computation.22 | async-start | bytes 1392640 | tf_op jit(solution)/shard_map/all_gather | solution.py:41
  551.9 70.1 %all-gather.37.cloned.1.call-start = ((), (), s32[]{:S(2)}) async-start(), calls=%async_computation.23 | async-start | bytes 4177920 | tf_op jit(solution)/shard_map/all_gather | solution.py:37
  557.6 13.4 %copy-start.6 = (bf16[512,1088]{0,1:T(8,128)(2,1)S(1)}, bf16[512,1088]{0,1:T(8,128)(2,1)}, u32[]{:S(2)}) copy-start(bf16[512,1088]{0,1:T(8,128)(2,1)} %all-gather.21.cloned.1.call-done) | copy-start | bytes 3342340
  569.1 4.1 copy-start.15
  585.6 5.0 copy-start.20
  585.6 5.0 copy-start.21
  591.7 158.4 %reduce-scatter.13.cloned.1.call-start = ((), (), s32[]{:S(2)}) async-start(), calls=%async_computation.26 | async-start | bytes 7520256
  599.5 1.9 copy-start.19
  599.5 253.8 %reduce-scatter.17.cloned.1.call-start = ((), (), s32[]{:S(2)}) async-start(), calls=%async_computation.28 | async-start | bytes 5640192
  605.3 316.1 %reduce-scatter.15.cloned.1.call-start = ((), (), s32[]{:S(2)}) async-start(), calls=%async_computation.27 | async-start | bytes 1880064
  608.5 415.5 %reduce-scatter.11.cloned.1.call-start = ((), (), s32[]{:S(2)}) async-start(), calls=%async_computation.24 | async-start | bytes 5640192 | tf_op jit(solution)/shard_map/reduce_scatter | solution.py:232
  628.2 1.9 copy-start
  634.0 8.6 copy-start.35
  634.0 9.0 copy-start.29
  634.0 9.1 copy-start.28
  634.0 9.2 copy-start.30
  634.0 17.7 %copy-start.3 = (bf16[128,1088]{0,1:T(8,128)(2,1)S(1)}, bf16[128,1088]{0,1:T(8,128)(2,1)}, u32[]{:S(2)}) copy-start(bf16[128,1088]{0,1:T(8,128)(2,1)} %param.8) | copy-start | bytes 835588
  634.0 17.7 %copy-start.32 = (f32[128]{0:T(128)S(1)}, f32[128]{0:T(128)}, u32[]{:S(2)}) copy-start(f32[128]{0:T(128)} %copy-done.31) | copy-start | bytes 1540
  634.0 17.7 %copy-start.39 = (f32[128]{0:T(128)S(1)}, f32[128]{0:T(128)}, u32[]{:S(2)}) copy-start(f32[128]{0:T(128)} %copy-done.38) | copy-start | bytes 1540
  638.9 13.8 %copy-start.14 = (f32[128,1088]{0,1:T(8,128)S(1)}, f32[128,1088]{0,1:T(8,128)}, u32[]{:S(2)}) copy-start(f32[128,1088]{0,1:T(8,128)} %get-tuple-element.16) | copy-start | bytes 1671172
  638.9 12.8 %all-to-all-start.7 = ((f32[4,128,272]{1,2,0:T(8,128)}), f32[4,128,272]{1,2,0:T(8,128)S(1)}, u32[]{:S(2)}, u32[]{:S(2)}) async-start(f32[4,128,272]{1,2,0:T(8,128)} %fusion.33), calls=%async_computation.7 | async-start | bytes 1114112 | tf_op jit(solution)/shard_map/all_to_all | solution.py:45
  (5 other events, 6.0 us)
Sparse Core Ops, SparseCore 0:
  10.2 57.2 all-gather.16
  69.7 15.7 all-gather.14
  132.4 28.4 all-gather.18
  168.7 17.2 all-gather.20
  188.0 56.4 all-gather.38
  263.7 17.4 all-gather.22
  282.7 17.2 all-gather.28
  302.2 53.5 all-gather.26
  395.0 36.1 all-gather.30
  432.6 57.0 all-gather.24
  531.7 17.6 all-gather.32
  552.0 17.0 all-gather.34
  591.9 30.0 all-gather.36
  625.4 124.6 reduce-scatter.12
  754.2 98.9 reduce-scatter.16
  857.6 63.6 reduce-scatter.14
  925.4 98.5 reduce-scatter.10
where the time goes:
time: 1040 us; the launch traced here: 1030 us
  waiting for transfers between devices  536 us (52%)
  local copies, waits for them, and re-layouts  161 us (15%)
  blocking collectives  149 us (14%)
  matrix products  75.7 us (7%)
  other arithmetic  71.4 us (7%)
  starting transfers between devices  23 us (2%)
  between operations  15.1 us (1%)
    unnamed x20, waiting for transfers between devices  224 us
    reduce_scatter x1, waiting for transfers between devices, body(): lax.psum_scatter(attend_grad, 'dp', scatter_dimension=2, tiled=True)  103 us
    unnamed x2, blocking collectives  86.5 us
    unnamed x3, other arithmetic  52.1 us
    all_to_all x1, waiting for transfers between devices, body(): lax.all_to_all(shrink_rows[:, None, :], 'seq', split_axis=2, concat_axis=...  49.3 us
    unnamed x105, local copies, waits for them, and re-layouts  44.2 us
    all_to_all x1, waiting for transfers between devices, body(): lax.all_to_all(attend_rows, 'seq', split_axis=2, concat_axis=0, tiled=True)  38.6 us
    all_gather x1, blocking collectives, body(): lax.all_gather(output_weight, 'dp', axis=1, tiled=True)  32.6 us
  transfers between devices with their start and end apart: 23, of which 14 were waited for; matrix products, arithmetic and copies ran while one was open for 24% of the time, Pallas kernels for 0%

commit v1 on v0

v1 whole, which is shorter than its diff:
```python
import math
import jax
import jax.numpy as jnp
from jax import lax
from jax.sharding import PartitionSpec as P

D = 1088
H = 17
HD = 64
FF = 4352
EPS = 1e-05
BF = jnp.bfloat16
F32 = jnp.float32


def layer_norm(values):
    centre = values - jnp.mean(values, axis=-1, keepdims=True)
    inverse = lax.rsqrt(jnp.mean(centre * centre, axis=-1, keepdims=True) + EPS)
    return (centre * inverse, inverse)


def norm_back(upstream, normed, inverse, gain):
    scaled = upstream * gain
    return (
        scaled
        - jnp.mean(scaled, axis=-1, keepdims=True)
        - normed * jnp.mean(scaled * normed, axis=-1, keepdims=True)
    ) * inverse


def gelu_parts(pre):
    normal_cdf = 0.5 * (1.0 + lax.erf(pre * 0.7071067811865476))
    density = jnp.exp(-0.5 * pre * pre) * 0.3989422804014327
    return (pre * normal_cdf, normal_cdf + pre * density)


def gather_seq(values):
    return lax.all_gather(values, "seq", axis=0, tiled=False)


def gather_dp(values):
    return lax.all_gather(values, "dp", axis=0, tiled=False)


def swap_seq(values):
    return lax.all_to_all(values, "seq", split_axis=0, concat_axis=0, tiled=True)


def sum_seq(values):
    return lax.psum_scatter(values, "seq", scatter_dimension=0, tiled=False).astype(F32)


def sum_dp(values):
    return lax.psum_scatter(values, "dp", scatter_dimension=0, tiled=False).astype(F32)


def dot(a, b, ca, cb):
    return lax.dot_general(a, b, (((ca,), (cb,)), ((), ())), preferred_element_type=F32)


def up(value, step):
    return -(-value // step) * step


def padded(values, shape):
    return jnp.pad(values, [(0, n - m) for m, n in zip(values.shape, shape)])


def body(
    tokens,
    segment_ids,
    attend_weight,
    output_weight,
    expand_weight,
    shrink_weight,
    vectors,
    cotangent,
):
    rows = tokens.shape[0]
    S = lax.axis_size("seq")
    N = lax.axis_size("dp")
    group = rows * S
    place = lax.axis_index("seq")
    dr = D // S
    dc = D // N
    fc = FF // N
    hq = FF // S
    heads = -(-H // S)
    hw = heads * HD
    vn = vectors.shape[0]
    row_pad = up(dr, 16)
    cols = 12 * dc
    col_pad = up(cols, 128)

    shrink_split = shrink_weight.reshape(4, dr, dc).transpose(1, 0, 2).reshape(dr, 4 * dc)
    packed = jnp.concatenate(
        (expand_weight, attend_weight.reshape(dr, 3 * dc), output_weight, shrink_split), axis=1
    )
    packed = padded(packed, (row_pad, col_pad))
    packed = jnp.concatenate((packed, padded(vectors[None], (16, col_pad))), axis=0)
    whole = gather_dp(packed)
    both = gather_seq(jnp.concatenate((tokens, cotangent), axis=1))
    tokens_all = both[:, :, :D].reshape(group, D)
    upstream_all = both[:, :, D:].reshape(group, D)

    mine = whole[:, :dr]
    expand_rows = mine[:, :, : 4 * dc].transpose(1, 0, 2).reshape(dr, FF)
    attend_rows = (
        mine[:, :, 4 * dc : 7 * dc].reshape(N, dr, 3, dc).transpose(1, 2, 0, 3).reshape(dr, 3, D)
    )
    output_rows = mine[:, :, 7 * dc : 8 * dc].transpose(1, 0, 2).reshape(dr, D)
    shrink_rows = (
        mine[:, :, 8 * dc : 12 * dc].reshape(N, dr, 4, dc).transpose(2, 1, 0, 3).reshape(4 * dr, D)
    )

    attend_out = (
        padded(attend_rows, (dr, 3, S * hw)).reshape(dr, 3, S, hw).transpose(2, 0, 1, 3)
    ).reshape(S, dr, 3 * hw)
    attend_cols = swap_seq(attend_out).reshape(D, 3 * hw)
    expand_out = expand_rows.reshape(dr, S, hq).transpose(1, 0, 2)
    expand_cols = swap_seq(expand_out).reshape(D, hq)
    output_and = jnp.concatenate(
        (padded(output_rows, (row_pad, D)), padded(whole[:, row_pad, :vn], (up(N, 16), D))), axis=0
    )
    output_and_all = gather_seq(output_and)
    output_all = output_and_all[:, :dr].reshape(D, D)
    output_heads = lax.dynamic_slice_in_dim(
        padded(output_all, (S * hw, D)), place * hw, hw, 0
    )
    flat = output_and_all[:, row_pad : row_pad + N, :vn].transpose(1, 0, 2).reshape(-1)
    table = flat[: 8 * D].astype(F32).reshape(8, D)
    fc_bias = flat[8 * D :].astype(F32)

    def head_part(vector):
        return lax.dynamic_slice_in_dim(padded(vector, (S * hw,)), place * hw, hw, 0)

    normed_all, _ = layer_norm(tokens_all.astype(F32))
    hidden_one_all = (normed_all * table[0] + table[1]).astype(BF)
    inputs32 = tokens.astype(F32)
    normed_one, inverse_one = layer_norm(inputs32)
    projected = dot(hidden_one_all, attend_cols, 1, 0)
    bias = jnp.concatenate((head_part(table[2]), jnp.zeros((hw,), F32), head_part(table[3])))
    triple = (projected + bias).astype(BF).reshape(group, 3, heads, HD).transpose(1, 2, 0, 3)
    query, key, value = triple[0], triple[1], triple[2]
    segment = segment_ids.reshape(-1)
    pos = jnp.arange(group, dtype=jnp.int32)
    allowed = (pos[None, :] <= pos[:, None]) & (segment[None, :] == segment[:, None])
    scores = jnp.einsum("htd,hgd->htg", query, key, preferred_element_type=F32) * 0.125
    scores = jnp.where(allowed[None], scores, -jnp.inf)
    peak = jnp.max(scores, axis=-1, keepdims=True)
    unscaled = jnp.exp(scores - peak)
    probs = unscaled / jnp.sum(unscaled, axis=-1, keepdims=True)
    probs_low = probs.astype(BF)
    context = jnp.einsum("htg,hgd->htd", probs_low, value, preferred_element_type=F32).astype(BF)
    context_cols = context.transpose(1, 0, 2).reshape(group, hw)
    attn = dot(context_cols, output_heads, 1, 0).astype(BF)
    residual = inputs32 + sum_seq(attn.reshape(S, rows, D)) + table[4]
    normed_two, inverse_two = layer_norm(residual)
    hidden_two = (normed_two * table[5] + table[6]).astype(BF)
    hidden_two_all = gather_seq(hidden_two).reshape(group, D)
    hidden_bias = lax.dynamic_slice_in_dim(fc_bias, place * hq, hq, 0)
    pre = dot(hidden_two_all, expand_cols, 1, 0) + hidden_bias
    activated, slope = gelu_parts(pre)
    activated_low = activated.astype(BF)
    branch = dot(activated_low, shrink_rows, 1, 0).astype(BF)
    upstream = cotangent.astype(F32)
    pre_grad = dot(upstream_all, shrink_rows, 1, 1) * slope
    pre_low = pre_grad.astype(BF)
    hidden_two_grad = sum_seq(dot(pre_low, expand_cols, 1, 1).astype(BF).reshape(S, rows, D))
    mixed = (residual + sum_seq(branch.reshape(S, rows, D)) + table[7]).astype(BF)
    shrink_grad = dot(activated_low, upstream_all, 0, 0).astype(BF)
    expand_grad = dot(hidden_two_all, pre_low, 0, 0).astype(BF)
    expand_grad = swap_seq(expand_grad.reshape(S, dr, hq))
    residual_grad = upstream + norm_back(hidden_two_grad, normed_two, inverse_two, table[5])
    residual_all = gather_seq(residual_grad.astype(BF)).reshape(group, D)
    grad = dot(residual_all, output_heads, 1, 1).astype(BF)
    grad = grad.reshape(group, heads, HD).transpose(1, 0, 2)
    row_dots = jnp.sum(grad.astype(F32) * context.astype(F32), axis=-1, keepdims=True)
    prob_grad = jnp.einsum("htd,hgd->htg", grad, value, preferred_element_type=F32)
    score_grad = (probs * (prob_grad - row_dots)).astype(BF)
    query_grad = jnp.einsum("htg,hgd->thd", score_grad, key, preferred_element_type=F32) * 0.125
    key_grad = jnp.einsum("htg,htd->ghd", score_grad, query, preferred_element_type=F32) * 0.125
    value_grad = jnp.einsum("htg,htd->ghd", probs_low, grad, preferred_element_type=F32)
    query_grad, key_grad, value_grad = (
        g.reshape(group, hw) for g in (query_grad, key_grad, value_grad)
    )
    joined = jnp.concatenate((query_grad, key_grad, value_grad), axis=1).astype(BF)
    hidden_one_grad = sum_seq(dot(joined, attend_cols, 1, 1).astype(BF).reshape(S, rows, D))
    attend_grad = dot(hidden_one_all, joined, 0, 0).astype(BF)
    attend_grad = swap_seq(attend_grad.reshape(S, dr, 3 * hw))
    output_grad = dot(context_cols, residual_all, 0, 0).astype(BF)
    output_grad = lax.dynamic_slice_in_dim(
        gather_seq(output_grad).reshape(S * hw, D), place * dr, dr, 0
    )
    tokens_grad = residual_grad + norm_back(hidden_one_grad, normed_one, inverse_one, table[0])

    attend_grad = attend_grad.reshape(S, dr, 3, hw).transpose(1, 2, 0, 3).reshape(dr, 3, S * hw)
    attend_grad = attend_grad[:, :, :D].reshape(dr, 3, N, dc).transpose(2, 0, 1, 3)
    expand_grad = expand_grad.reshape(S, dr, N // S, fc).transpose(0, 2, 1, 3).reshape(N, dr, fc)
    output_grad = output_grad.reshape(dr, N, dc).transpose(1, 0, 2)
    shrink_grad = shrink_grad.reshape(4, dr, N, dc).transpose(2, 1, 0, 3).reshape(N, dr, 4 * dc)
    packed_grad = jnp.concatenate(
        (expand_grad, attend_grad.reshape(N, dr, 3 * dc), output_grad, shrink_grad), axis=2
    )

    def spread(vector, total, start):
        return lax.dynamic_update_slice(jnp.zeros((total,), F32), vector, (start,))

    vector_grad = jnp.concatenate(
        (
            jnp.sum(hidden_one_grad * normed_one, axis=0),
            jnp.sum(hidden_one_grad, axis=0),
            spread(jnp.sum(query_grad, axis=0), S * hw, place * hw)[:D],
            spread(jnp.sum(value_grad, axis=0), S * hw, place * hw)[:D],
            jnp.sum(residual_grad, axis=0),
            jnp.sum(hidden_two_grad * normed_two, axis=0),
            jnp.sum(hidden_two_grad, axis=0),
            jnp.sum(upstream, axis=0),
            spread(jnp.sum(pre_grad, axis=0), FF, place * hq),
        )
    )
    by_owner = vector_grad.reshape(N, S, vn).transpose(1, 0, 2)
    by_owner = padded(by_owner, (S, up(N, 16), up(vn, 128)))
    vector_part = sum_seq(by_owner)[:N].astype(BF)
    vector_part = padded(vector_part[:, None, :], (N, 16, col_pad))
    packed_grad = jnp.concatenate(
        (padded(packed_grad, (N, row_pad, col_pad)), vector_part), axis=1
    )
    total = sum_dp(packed_grad)
    weight_sum = total[:dr]
    return (
        mixed,
        tokens_grad,
        weight_sum[:, 4 * dc : 7 * dc].reshape(dr, 3, dc),
        weight_sum[:, 7 * dc : 8 * dc],
        weight_sum[:, : 4 * dc],
        weight_sum[:, 8 * dc : 12 * dc].reshape(dr, 4, dc).transpose(1, 0, 2).reshape(4 * dr, dc),
        total[row_pad, :vn],
    )


def solution(mesh):
    return jax.shard_map(
        body,
        mesh=mesh,
        in_specs=(
            P(("dp", "seq"), None),
            P("dp", None),
            P("seq", None, "dp"),
            P("seq", "dp"),
            P("seq", "dp"),
            P("seq", "dp"),
            P(("dp", "seq")),
            P(("dp", "seq"), None),
        ),
        out_specs=(
            P(("dp", "seq"), None),
            P(("dp", "seq"), None),
            P("seq", None, "dp"),
            P("seq", "dp"),
            P("seq", "dp"),
            P("seq", "dp"),
            P(("dp", "seq")),
        ),
        check_vma=False,
    )
```

time: 1040 us -> 730 us (0.70)
  blocking collectives: 149 us -> 0 us
  waiting for transfers between devices: 536 us -> 424 us
  other arithmetic: 71.4 us -> 39.9 us
  matrix products: 75.7 us -> 54.5 us
    unnamed x20 -> x12, waiting for transfers between devices: 224 us -> 0.2 us
    reduce_scatter x1 -> x6, waiting for transfers between devices: 103 us -> 211 us  [the longest x1 137 us: sum_dp(): lax.psum_scatter(values, 'dp', scatter_dimension=0, tiled=False).astype(F32)]
    unnamed x2 -> x0, blocking collectives: 86.5 us -> none
    all_gather x13 -> x6, waiting for transfers between devices: 78.6 us -> 154 us  [the longest x1 118 us: gather_dp(): return lax.all_gather(values, 'dp', axis=0, tiled=False)]
    all_to_all x6 -> x4, waiting for transfers between devices: 131 us -> 58.5 us  [swap_seq(): lax.all_to_all(values, 'seq', split_axis=0, concat_axis=0, tiled=True)]
    unnamed x3 -> x0, other arithmetic: 52.1 us -> none
    broadcast_in_dim x4 -> x3, local copies, waits for them, and re-layouts: 47.1 us -> 0.86 us  [the longest x1 0.85 us: body(): vectors[None]]
    reshape x3 -> x17, local copies, waits for them, and re-layouts: 3.62 us -> 47.5 us  [the longest x2 12.1 us: body(): shrink_grad.reshape(4, dr, N, dc).transpose(2, 1, 0, 3)]
  transfers between devices with their start and end apart: 23 -> 16, of which waited for: 14 -> 11; matrix products, arithmetic and copies ran while one was open for 24% -> 23% of each run, Pallas kernels for 0% -> 0%
where the time goes in v1:
time: 730 us; the launch traced here: 721 us
  waiting for transfers between devices  424 us (58%)
  local copies, waits for them, and re-layouts  169 us (23%)
  matrix products  54.5 us (7%)
  other arithmetic  39.9 us (5%)
  starting transfers between devices  18.9 us (3%)
  between operations  15.4 us (2%)
    reduce_scatter x1, waiting for transfers between devices, sum_dp(): lax.psum_scatter(values, 'dp', scatter_dimension=0, tiled=False).astype(F32)  137 us
    all_gather x1, waiting for transfers between devices, gather_dp(): return lax.all_gather(values, 'dp', axis=0, tiled=False)  118 us
    reduce_scatter x5, waiting for transfers between devices, sum_seq(): lax.psum_scatter(values, 'seq', scatter_dimension=0, tiled=False)  74.4 us
    all_to_all x4, waiting for transfers between devices, swap_seq(): lax.all_to_all(values, 'seq', split_axis=0, concat_axis=0, tiled=True)  58.5 us
    dot_general x12, matrix products, dot(): lax.dot_general(a, b, (((ca,), (cb,)), ((), ())), preferred_element_type=...  40.7 us
    all_gather x5, waiting for transfers between devices, gather_seq(): return lax.all_gather(values, 'seq', axis=0, tiled=False)  35.7 us
    all_to_all x4, starting transfers between devices, swap_seq(): lax.all_to_all(values, 'seq', split_axis=0, concat_axis=0, tiled=True)  17.3 us
  transfers between devices with their start and end apart: 16, of which 11 were waited for; matrix products, arithmetic and copies ran while one was open for 23% of the time, Pallas kernels for 0%

profile of v1, /device:TPU:0, one launch (start us, length us, event | category | flops | bytes accessed | tf_op | source)
XLA Modules:
  0.0 721.1 jit_solution(16488778843071157206)
XLA Ops:
  11.1 2.3 copy.107
  14.4 117.9 %all-gather.15.cloned.1.call-done = bf16[2304,1664]{1,0:T(8,128)(2,1)} async-done(((bf16[288,1664]{1,0:T(8,128)(2,1)}), bf16[2304,1664]{1,0:T(8,128)(2,1)}) %all-gather.15.cloned.1.call-update) | async-done | bytes 7667728 | tf_op jit(solution)/shard_map/all_gather | solution.py:42
  133.3 2.0 slice_bitcast_fusion.1
  137.6 18.6 %all-gather.13.cloned.1.call-done = bf16[512,2176]{0,1:T(8,128)(2,1)} async-done(((bf16[128,2176]{0,1:T(8,128)(2,1)}), bf16[512,2176]{0,1:T(8,128)(2,1)}) %all-gather.13.cloned.1.call-update) | async-done | bytes 2228240 | tf_op jit(solution)/shard_map/all_gather | solution.py:38
  156.2 4.0 reshape.373
  163.2 4.6 slice.161
  167.8 4.4 copy.112
  172.2 2.0 copy.113
  176.1 7.1 copy.153
  183.3 7.1 copy.115
  190.4 4.4 copy.116
  194.8 4.5 all-to-all-start
  200.4 3.4 slice.167
  205.0 5.0 add_convert_fusion
  210.0 16.5 %all-to-all-done = bf16[4,272,960]{2,1,0:T(8,128)(2,1)} async-done(((bf16[4,272,960]{2,1,0:T(8,128)(2,1)}), bf16[4,272,960]{2,1,0:T(8,128)(2,1)}, u32[]{:S(2)}, u32[]{:S(2)}) %all-to-all-start) | async-done | bytes 2088992 | tf_op jit(solution)/shard_map/all_to_all | solution.py:46
  226.4 4.4 add_convert_fusion.1
  230.8 5.4 fusion.95
  236.2 3.2 fusion.21
  244.3 5.9 slice_bitcast_fusion
  250.2 2.2 copy.119
  252.3 6.0 reshape_reshape.3
  258.4 3.5 copy.120
  261.9 4.5 all-to-all-start.1
  266.5 3.2 reduce-scatter.7.cloned.1.call-done
  272.1 2.2 add_convert_fusion.2
  276.4 4.7 copy.121
  281.1 5.1 copy.122
  286.2 5.1 reshape.344
  291.4 11.1 %all-to-all-done.1 = bf16[4,272,1088]{2,1,0:T(8,128)(2,1)} async-done(((bf16[4,272,1088]{2,1,0:T(8,128)(2,1)}), bf16[4,272,1088]{2,1,0:T(8,128)(2,1)}, u32[]{:S(2)}, u32[]{:S(2)}) %all-to-all-start.1) | async-done | bytes 2367520 | tf_op jit(solution)/shard_map/all_to_all | solution.py:46
  302.5 5.0 multiply_convert_fusion.1
  307.6 3.6 fusion.96
  311.2 3.7 fusion.26
  316.2 2.9 fusion.25
  320.4 21.1 %reduce-scatter.11.cloned.1.call-done = bf16[1,128,1088]{1,2,0:T(8,128)(2,1)} async-done(((bf16[4,128,1088]{1,2,0:T(8,128)(2,1)}), bf16[1,128,1088]{1,2,0:T(8,128)(2,1)}) %reduce-scatter.11.cloned.1.call-update) | async-done | bytes 278544 | tf_op jit(solution)/shard_map/reduce_scatter | solution.py:50
  341.5 2.1 fusion.68
  343.6 25.8 %reduce-scatter.9.cloned.1.call-done = bf16[1,128,1088]{1,2,0:T(8,128)(2,1)} async-done(((bf16[4,128,1088]{1,2,0:T(8,128)(2,1)}), bf16[1,128,1088]{1,2,0:T(8,128)(2,1)}) %reduce-scatter.9.cloned.1.call-update) | async-done | bytes 278544 | tf_op jit(solution)/shard_map/reduce_scatter | solution.py:50
  369.4 2.9 fusion.89
  374.1 17.1 %all-gather.21.cloned.1.call-done = bf16[512,1088]{0,1:T(8,128)(2,1)} async-done(((bf16[128,1088]{0,1:T(8,128)(2,1)}), bf16[512,1088]{0,1:T(8,128)(2,1)}) %all-gather.21.cloned.1.call-update) | async-done | bytes 1114128 | tf_op jit(solution)/shard_map/all_gather | solution.py:38
  391.2 2.1 convolution_convert_fusion.8
  395.1 3.4 multiply_convert_fusion
  400.0 3.1 fusion.24
  405.7 24.3 %reduce-scatter.13.cloned.1.call-done = bf16[1,128,1088]{1,2,0:T(8,128)(2,1)} async-done(((bf16[4,128,1088]{1,2,0:T(8,128)(2,1)}), bf16[1,128,1088]{1,2,0:T(8,128)(2,1)}) %reduce-scatter.13.cloned.1.call-update) | async-done | bytes 278544 | tf_op jit(solution)/shard_map/reduce_scatter | solution.py:50
  435.6 4.3 convolution_convert_fusion.1
  439.9 3.8 all-to-all-start.2
  443.8 4.6 convolution_convert_fusion.2
  448.4 4.2 copy.130
  452.6 30.9 %all-to-all-done.2 = bf16[4,272,1088]{2,1,0:T(8,128)(2,1)S(1)} async-done(((bf16[4,272,1088]{2,1,0:T(8,128)(2,1)}), bf16[4,272,1088]{2,1,0:T(8,128)(2,1)S(1)}, u32[]{:S(2)}, u32[]{:S(2)}) %all-to-all-start.2) | async-done | bytes 2367520 | tf_op jit(solution)/shard_map/all_to_all | solution.py:46
  483.5 4.5 all-to-all-start.3
  488.3 4.7 convolution_convert_fusion
  493.0 5.1 copy.137
  498.1 7.3 %reshape.363 = bf16[4,272,8,136]{1,0,3,2:T(4,128)(2,1)} reshape(bf16[1088,1088]{0,1:T(8,128)(2,1)} %copy.137) | data formatting | bytes 4734976 | tf_op jit(solution)/shard_map/reshape | solution.py:201
  505.5 4.1 copy.138
  509.6 4.7 copy.140
  516.8 3.3 copy.131
  520.1 5.2 copy.132
  525.3 4.4 reshape.358
  531.2 2.9 copy.133
  535.8 4.4 copy.139
  541.0 2.1 constant_dynamic-slice_fusion
  543.1 2.3 copy.135
  545.3 2.4 copy.136
  547.8 13.2 %concatenate.38 = bf16[8,272,1632]{2,1,0:T(8,128)(2,1)} concatenate(bf16[8,272,544]{2,1,0:T(8,128)(2,1)} %bitcast.262, bf16[8,272,408]{2,1,0:T(8,128)(2,1)} %copy.139, bf16[8,272,136]{2,1,0:T(8,128)(2,1)} %bitcast.280, bf16[8,272,544]{2,1,0:T(8,128)(2,1)S(1)} %copy-done.4), dimensions={2} | concatenate | bytes 14204928 | tf_op jit(solution)/shard_map/concatenate | solution.py:202
  561.0 6.6 fusion.3
  569.8 137.1 %reduce-scatter.17.cloned.1.call-done = bf16[1,288,1664]{2,1,0:T(8,128)(2,1)} async-done(((bf16[8,288,1664]{2,1,0:T(8,128)(2,1)}), bf16[1,288,1664]{2,1,0:T(8,128)(2,1)}) %reduce-scatter.17.cloned.1.call-update) | async-done | bytes 958480 | tf_op jit(solution)/shard_map/reduce_scatter | solution.py:54
  (202 shorter events, 56.2 us)
Async XLA Ops:
  7.2 3.6 copy-start.22
  7.2 3.6 copy-start.17
  7.2 125.1 %all-gather.15.cloned.1.call-start = ((), (), s32[]{:S(2)}) async-start(), calls=%async_computation.17 | async-start | bytes 8626176 | tf_op jit(solution)/shard_map/all_gather | solution.py:42
  11.1 2.4 copy-start.3
  11.1 2.4 copy-start.11
  13.4 142.8 %all-gather.13.cloned.1.call-start = ((), (), s32[]{:S(2)}) async-start(), calls=%async_computation.16 | async-start | bytes 2785280 | tf_op jit(solution)/shard_map/all_gather | solution.py:38
  14.4 186.0 %all-gather.17.cloned.1.call-start = ((), (), s32[]{:S(2)}) async-start(), calls=%async_computation.18 | async-start | bytes 3317760 | tf_op jit(solution)/shard_map/all_gather | solution.py:38
  136.1 1.3 copy-start.31
  194.8 31.7 %all-to-all-start = ((bf16[4,272,960]{2,1,0:T(8,128)(2,1)}), bf16[4,272,960]{2,1,0:T(8,128)(2,1)}, u32[]{:S(2)}, u32[]{:S(2)}) async-start(bf16[4,272,960]{2,1,0:T(8,128)(2,1)} %copy.116), calls=%async_computation | async-start | bytes 4456448 | tf_op jit(solution)/shard_map/all_to_all | solution.py:46
  199.3 70.4 %reduce-scatter.7.cloned.1.call-start = ((), (), s32[]{:S(2)}) async-start(), calls=%async_computation.10 | async-start | bytes 1392640 | tf_op jit(solution)/shard_map/reduce_scatter | solution.py:50
  204.8 26.1 %copy-start.18 = (f32[1088]{0:T(1024)}, f32[1088]{0:T(1024)S(1)}, u32[]{:S(2)}) copy-start(f32[1088]{0:T(1024)S(1)} %get-tuple-element.66) | copy-start | bytes 13060
  204.8 26.1 %copy-start.23 = (f32[1088]{0:T(1024)}, f32[1088]{0:T(1024)S(1)}, u32[]{:S(2)}) copy-start(f32[1088]{0:T(1024)S(1)} %get-tuple-element.65) | copy-start | bytes 13060
  236.2 3.2 copy-start.28
  239.4 3.6 copy-start
  239.4 2.8 copy-start.2
  261.9 40.7 %all-to-all-start.1 = ((bf16[4,272,1088]{2,1,0:T(8,128)(2,1)}), bf16[4,272,1088]{2,1,0:T(8,128)(2,1)}, u32[]{:S(2)}, u32[]{:S(2)}) async-start(bf16[4,272,1088]{2,1,0:T(8,128)(2,1)} %copy.120), calls=%async_computation.2 | async-start | bytes 5013504 | tf_op jit(solution)/shard_map/all_to_all | solution.py:46
  266.4 36.1 %all-gather.19.cloned.1.call-start = ((), (), s32[]{:S(2)}) async-start(), calls=%async_computation.19 | async-start | bytes 1392640 | tf_op jit(solution)/shard_map/all_gather | solution.py:38
  274.3 67.3 %reduce-scatter.11.cloned.1.call-start = ((), (), s32[]{:S(2)}) async-start(), calls=%async_computation.12 | async-start | bytes 1392640 | tf_op jit(solution)/shard_map/reduce_scatter | solution.py:50
  302.5 5.0 copy-start.12
  311.2 3.7 copy-start.44
  316.1 53.2 %reduce-scatter.9.cloned.1.call-start = ((), (), s32[]{:S(2)}) async-start(), calls=%async_computation.11 | async-start | bytes 1392640 | tf_op jit(solution)/shard_map/reduce_scatter | solution.py:50
  319.0 22.5 %copy-start.5 = (bf16[1,128,1088]{1,2,0:T(8,128)(2,1)S(1)}, bf16[1,128,1088]{1,2,0:T(8,128)(2,1)}, u32[]{:S(2)}) copy-start(bf16[1,128,1088]{1,2,0:T(8,128)(2,1)} %reduce-scatter.7.cloned.1.call-done) | copy-start | bytes 835588
  320.3 70.9 %all-gather.21.cloned.1.call-start = ((), (), s32[]{:S(2)}) async-start(), calls=%async_computation.20 | async-start | bytes 1392640 | tf_op jit(solution)/shard_map/all_gather | solution.py:38
  343.6 28.7 %copy-start.33 = (f32[128]{0:T(128)}, f32[128]{0:T(128)S(1)}, u32[]{:S(2)}) copy-start(f32[128]{0:T(128)S(1)} %broadcast_multiply_fusion.2) | copy-start | bytes 1540
  372.3 0.8 copy-start.6
  373.9 19.5 %copy-start.1 = (bf16[5,512,512]{1,2,0:T(8,128)(2,1)S(1)}, bf16[5,512,512]{1,2,0:T(8,128)(2,1)}, u32[]{:S(2)}) copy-start(bf16[5,512,512]{1,2,0:T(8,128)(2,1)} %copy-done) | copy-start | bytes 7864324
  373.9 56.1 %reduce-scatter.13.cloned.1.call-start = ((), (), s32[]{:S(2)}) async-start(), calls=%async_computation.13 | async-start | bytes 1392640 | tf_op jit(solution)/shard_map/reduce_scatter | solution.py:50
  393.3 1.7 copy-start.13
  393.3 1.7 copy-start.29
  399.4 3.7 copy-start.14
  400.0 3.1 copy-start.16
  403.1 1.4 copy-start.32
  403.1 1.7 copy-start.10
  403.2 1.9 copy-start.42
  403.2 1.9 copy-start.30
  403.2 27.9 %copy-start.19 = (f32[1088]{0:T(1024)S(1)}, f32[1088]{0:T(1024)}, u32[]{:S(2)}) copy-start(f32[1088]{0:T(1024)} %copy-done.18) | copy-start | bytes 13060
  403.2 27.9 %copy-start.34 = (f32[128]{0:T(128)S(1)}, f32[128]{0:T(128)}, u32[]{:S(2)}) copy-start(f32[128]{0:T(128)} %copy-done.33) | copy-start | bytes 1540
  403.2 29.8 %copy-start.25 = (f32[1088]{0:T(1024)S(1)}, f32[1088]{0:T(1024)}, u32[]{:S(2)}) copy-start(f32[1088]{0:T(1024)} %get-tuple-element.35) | copy-start | bytes 13060
  403.2 29.8 %copy-start.26 = (f32[1088]{0:T(1024)S(1)}, f32[1088]{0:T(1024)}, u32[]{:S(2)}) copy-start(f32[1088]{0:T(1024)} %get-tuple-element.42) | copy-start | bytes 13060
  403.2 29.8 %copy-start.27 = (f32[1088]{0:T(1024)S(1)}, f32[1088]{0:T(1024)}, u32[]{:S(2)}) copy-start(f32[1088]{0:T(1024)} %get-tuple-element.57) | copy-start | bytes 13060
  403.2 30.8 %copy-start.8 = (bf16[512,1088]{0,1:T(8,128)(2,1)S(1)}, bf16[512,1088]{0,1:T(8,128)(2,1)}, u32[]{:S(2)}) copy-start(bf16[512,1088]{0,1:T(8,128)(2,1)} %all-gather.21.cloned.1.call-done) | copy-start | bytes 3342340
  404.5 135.7 %reduce-scatter.15.cloned.1.call-start = ((), (), s32[]{:S(2)}) async-start(), calls=%async_computation.14 | async-start | bytes 163840 | tf_op jit(solution)/shard_map/reduce_scatter | solution.py:50
  405.1 30.5 %copy-start.36 = (f32[128]{0:T(128)}, f32[128]{0:T(128)S(1)}, u32[]{:S(2)}) copy-start(f32[128]{0:T(128)S(1)} %add_rsqrt_fusion.1) | copy-start | bytes 1540
  405.7 29.9 %copy-start.43 = (bf16[512,1088]{0,1:T(8,128)(2,1)S(1)}, bf16[512,1088]{0,1:T(8,128)(2,1)}, u32[]{:S(2)}) copy-start(bf16[512,1088]{0,1:T(8,128)(2,1)} %all-gather.19.cloned.1.call-done) | copy-start | bytes 3342340
  434.0 107.0 %all-gather.23.cloned.1.call-start = ((), (), s32[]{:S(2)}) async-start(), calls=%async_computation.21 | async-start | bytes 3686400 | tf_op jit(solution)/shard_map/all_gather | solution.py:38
  439.9 3.8 copy-start.15
  439.9 3.8 copy-start.20
  439.9 3.8 copy-start.24
  439.9 3.8 copy-start.38
  439.9 3.9 copy-start.39
  439.9 43.5 %all-to-all-start.2 = ((bf16[4,272,1088]{2,1,0:T(8,128)(2,1)}), bf16[4,272,1088]{2,1,0:T(8,128)(2,1)S(1)}, u32[]{:S(2)}, u32[]{:S(2)}) async-start(bf16[4,272,1088]{2,1,0:T(8,128)(2,1)} %bitcast.287), calls=%async_computation.6 | async-start | bytes 5013504 | tf_op jit(solution)/shard_map/all_to_all | solution.py:46
  483.5 33.4 %all-to-all-start.3 = ((bf16[4,272,960]{2,1,0:T(8,128)(2,1)}), bf16[4,272,960]{2,1,0:T(8,128)(2,1)}, u32[]{:S(2)}, u32[]{:S(2)}) async-start(bf16[4,272,960]{2,1,0:T(8,128)(2,1)} %bitcast.273), calls=%async_computation.7 | async-start | bytes 4456448 | tf_op jit(solution)/shard_map/all_to_all | solution.py:46
  488.0 218.9 %reduce-scatter.17.cloned.1.call-start = ((), (), s32[]{:S(2)}) async-start(), calls=%async_computation.15 | async-start | bytes 8626176 | tf_op jit(solution)/shard_map/reduce_scatter | solution.py:54
  540.9 6.8 copy-start.4
  567.6 0.7 copy-start.41
  567.6 0.7 copy-start.40
  567.6 1.1 copy-start.7
  567.6 1.1 copy-start.9
  567.6 1.1 copy-start.21
  567.6 1.1 copy-start.35
  567.6 1.1 copy-start.37
Sparse Core Ops, SparseCore 0:
  13.6 118.6 all-gather.14
  134.4 21.7 all-gather.12
  158.4 25.7 all-gather.16
  244.4 25.2 reduce-scatter.6
  274.4 23.2 all-gather.18
  316.3 25.2 reduce-scatter.10
  344.0 25.2 reduce-scatter.8
  374.0 17.1 all-gather.20
  404.6 25.3 reduce-scatter.12
  434.1 19.9 reduce-scatter.14
  455.7 36.0 all-gather.22
  567.8 139.0 reduce-scatter.16

commit v2 on v1

--- a/solution.py
+++ b/solution.py
@@ -1,7 +1,10 @@
+import itertools
 import math
 import jax
 import jax.numpy as jnp
 from jax import lax
+from jax.experimental import pallas as pl
+from jax.experimental.pallas import tpu as pltpu
 from jax.sharding import PartitionSpec as P
 
 D = 1088
@@ -34,24 +37,293 @@
     return (pre * normal_cdf, normal_cdf + pre * density)
 
 
+MESH = pl.DeviceIdType.MESH
+IDS = itertools.count()
+LIMIT = 48 * 2**20
+
+
+def greet(targets):
+    barrier = pltpu.get_barrier_semaphore()
+    for target in targets:
+        pl.semaphore_signal(barrier, inc=1, device_id=target, device_id_type=MESH)
+    pl.semaphore_wait(barrier, len(targets))
+
+
+def send(src, dst, send_sem, recv_sem, target):
+    copy = pltpu.make_async_remote_copy(
+        src_ref=src,
+        dst_ref=dst,
+        send_sem=send_sem,
+        recv_sem=recv_sem,
+        device_id=target,
+        device_id_type=MESH,
+    )
+    copy.start()
+    return copy
+
+
+def run_kernel(kernel, out_shapes, scratch, *args):
+    return pl.pallas_call(
+        kernel,
+        out_shape=out_shapes,
+        in_specs=[pl.BlockSpec(memory_space=pltpu.VMEM)] * len(args),
+        out_specs=jax.tree.map(lambda _: pl.BlockSpec(memory_space=pltpu.VMEM), out_shapes),
+        scratch_shapes=scratch,
+        compiler_params=pltpu.CompilerParams(
+            collective_id=next(IDS), has_side_effects=True, vmem_limit_bytes=LIMIT
+        ),
+    )(*args)
+
+
+def dma(*shape):
+    return pltpu.SemaphoreType.DMA(shape)
+
+
+def gather_seq_steps(n, src, dst, local, sends, recvs):
+    chips = n // 2
+    me = lax.axis_index("seq")
+    x, core = me // 2, me % 2
+    other = {"seq": x * 2 + (1 - core)}
+    own = pltpu.make_async_copy(src, dst.at[me], local)
+    own.start()
+    across = []
+    for k in range(1, chips):
+        target = {"seq": lax.rem(x + k, chips) * 2 + core}
+        across.append(send(src, dst.at[me], sends.at[0, k], recvs.at[0, k], target))
+    inner = [send(src, dst.at[me], sends.at[1, 0], recvs.at[1, 0], other)]
+
+    def finish():
+        for k in range(1, chips):
+            across[k - 1].wait_recv()
+            slot = lax.rem(x + chips - k, chips) * 2 + core
+            inner.append(
+                send(dst.at[slot], dst.at[slot], sends.at[1, k], recvs.at[1, k], other)
+            )
+        for copy in inner:
+            copy.wait_recv()
+        for copy in across + inner:
+            copy.wait_send()
+        own.wait()
+
+    return finish
+
+
+def seq_partners(n):
+    me = lax.axis_index("seq")
+    x, core = me // 2, me % 2
+    chips = n // 2
+    return [{"seq": x * 2 + (1 - core)}] + [
+        {"seq": lax.rem(x + k, chips) * 2 + core} for k in range(1, chips)
+    ]
+
+
 def gather_seq(values):
-    return lax.all_gather(values, "seq", axis=0, tiled=False)
-
-
-def gather_dp(values):
-    return lax.all_gather(values, "dp", axis=0, tiled=False)
+    n = lax.axis_size("seq")
+
+    def kernel(src, dst, local, sends, recvs):
+        greet(seq_partners(n))
+        gather_seq_steps(n, src, dst, local, sends, recvs)()
+
+    return run_kernel(
+        kernel,
+        jax.ShapeDtypeStruct((n,) + values.shape, values.dtype),
+        [pltpu.SemaphoreType.DMA, dma(2, n // 2), dma(2, n // 2)],
+        values,
+    )
 
 
 def swap_seq(values):
-    return lax.all_to_all(values, "seq", split_axis=0, concat_axis=0, tiled=True)
+    n = lax.axis_size("seq")
+
+    def kernel(src, dst, local, sends, recvs):
+        me = lax.axis_index("seq")
+        greet([{"seq": lax.rem(me + k, n)} for k in range(1, n)])
+        own = pltpu.make_async_copy(src.at[me], dst.at[me], local)
+        own.start()
+        copies = []
+        for k in range(n - 1, 0, -1):
+            to = lax.rem(me + k, n)
+            copies.append(
+                send(src.at[to], dst.at[me], sends.at[k - 1], recvs.at[k - 1], {"seq": to})
+            )
+        for copy in copies:
+            copy.wait_recv()
+        for copy in copies:
+            copy.wait_send()
+        own.wait()
+
+    return run_kernel(
+        kernel,
+        jax.ShapeDtypeStruct(values.shape, values.dtype),
+        [pltpu.SemaphoreType.DMA, dma(n - 1), dma(n - 1)],
+        values,
+    )
 
 
 def sum_seq(values):
-    return lax.psum_scatter(values, "seq", scatter_dimension=0, tiled=False).astype(F32)
+    return jnp.sum(swap_seq(values).astype(F32), axis=0)
+
+
+def dp_layout():
+    n = lax.axis_size("dp")
+    wide = math.isqrt(n // 2)
+    return n // wide, wide
+
+
+def pieces(size, parts):
+    units = size // 16
+    edges = [units * i // parts * 16 for i in range(parts + 1)]
+    return [(a, b - a) for a, b in zip(edges, edges[1:])]
+
+
+def dp_partners(deep, wide):
+    me = lax.axis_index("dp")
+    z, y = me // wide, me % wide
+    return [{"dp": lax.rem(z + k, deep) * wide + y} for k in range(1, deep)] + [
+        {"dp": z * wide + lax.rem(y + k, wide)} for k in range(1, wide)
+    ]
+
+
+def gather_start(values, both):
+    n = lax.axis_size("seq")
+    deep, wide = dp_layout()
+    chunks = pieces(values.shape[0], 3)
+
+    def kernel(src, act, dst, act_dst, local, s_sends, s_recvs, z_send, z_recv, y_send, y_recv):
+        me = lax.axis_index("dp")
+        z, y = me // wide, me % wide
+        greet(dp_partners(deep, wide) + seq_partners(n))
+        finish = gather_seq_steps(n, act, act_dst, local.at[0], s_sends, s_recvs)
+        own = pltpu.make_async_copy(src, dst.at[me], local.at[1])
+        own.start()
+        first, second = {}, []
+        for c, (start, size) in enumerate(chunks):
+            part = pl.ds(start, size)
+            for k in range(1, deep):
+                to = {"dp": lax.rem(z + k, deep) * wide + y}
+                first[c, k] = send(
+                    src.at[part], dst.at[me, part], z_send.at[c, k], z_recv.at[c, k], to
+                )
+            for j in range(1, wide):
+                to = {"dp": z * wide + lax.rem(y + j, wide)}
+                second.append(
+                    send(
+                        src.at[part], dst.at[me, part], y_send.at[c, j, 0], y_recv.at[c, j, 0], to
+                    )
+                )
+        for c, (start, size) in enumerate(chunks):
+            part = pl.ds(start, size)
+            for k in range(1, deep):
+                first[c, k].wait_recv()
+                slot = lax.rem(z + deep - k, deep) * wide + y
+                for j in range(1, wide):
+                    to = {"dp": z * wide + lax.rem(y + j, wide)}
+                    block = dst.at[slot, part]
+                    second.append(
+                        send(block, block, y_send.at[c, j, k], y_recv.at[c, j, k], to)
+                    )
+        finish()
+        for copy in second:
+            copy.wait_recv()
+        for copy in list(first.values()) + second:
+            copy.wait_send()
+        own.wait()
+
+    m = len(chunks)
+    return run_kernel(
+        kernel,
+        (
+            jax.ShapeDtypeStruct((deep * wide,) + values.shape, values.dtype),
+            jax.ShapeDtypeStruct((n,) + both.shape, both.dtype),
+        ),
+        [dma(2), dma(2, n // 2), dma(2, n // 2)]
+        + [dma(m, deep), dma(m, deep), dma(m, wide, deep), dma(m, wide, deep)],
+        values,
+        both,
+    )
 
 
 def sum_dp(values):
-    return lax.psum_scatter(values, "dp", scatter_dimension=0, tiled=False).astype(F32)
+    deep, wide = dp_layout()
+    rows, cols = values.shape[1:]
+    chunks = pieces(rows, 3)
+
+    def kernel(src, out, y_buf, z_out, z_buf, y_send, y_recv, z_send, z_recv):
+        me = lax.axis_index("dp")
+        z, y = me // wide, me % wide
+        greet(dp_partners(deep, wide))
+        order = list(range(1, deep)) + [0]
+        first, second = {}, []
+        for c, (start, size) in enumerate(chunks):
+            part = pl.ds(start, size)
+            for k in order:
+                for j in range(1, wide):
+                    there = lax.rem(y + j, wide)
+                    first[c, k, j] = send(
+                        src.at[lax.rem(z + k, deep) * wide + there, part],
+                        y_buf.at[j - 1, k, part],
+                        y_send.at[c, j, k],
+                        y_recv.at[c, j, k],
+                        {"dp": z * wide + there},
+                    )
+        for c, (start, size) in enumerate(chunks):
+            part = pl.ds(start, size)
+            for k in order:
+                for j in range(1, wide):
+                    first[c, k, j].wait_recv()
+                block = lax.rem(z + k, deep) * wide + y
+
+                @pl.loop(0, size // 16)
+                def _(i):
+                    strip = pl.ds(pl.multiple_of(start + i * 16, 16), 16)
+                    total = src[block, strip, :].astype(F32)
+                    for j in range(1, wide):
+                        total = total + y_buf[j - 1, k, strip, :].astype(F32)
+                    if k == 0:
+                        out[strip, :] = total
+                    else:
+                        z_out[k - 1, strip, :] = total.astype(z_out.dtype)
+
+                if k > 0:
+                    second.append(
+                        send(
+                            z_out.at[k - 1, part],
+                            z_buf.at[k - 1, part],
+                            z_send.at[c, k],
+                            z_recv.at[c, k],
+                            {"dp": block},
+                        )
+                    )
+        for c, (start, size) in enumerate(chunks):
+            for k in range(1, deep):
+                second[c * (deep - 1) + k - 1].wait_recv()
+
+            @pl.loop(0, size // 16)
+            def _(i):
+                strip = pl.ds(pl.multiple_of(start + i * 16, 16), 16)
+                total = out[strip, :]
+                for k in range(1, deep):
+                    total = total + z_buf[k - 1, strip, :].astype(F32)
+                out[strip, :] = total
+
+        for copy in list(first.values()) + second:
+            copy.wait_send()
+
+    m = len(chunks)
+    return run_kernel(
+        kernel,
+        jax.ShapeDtypeStruct((rows, cols), F32),
+        [
+            pltpu.VMEM((wide - 1, deep, rows, cols), BF),
+            pltpu.VMEM((deep - 1, rows, cols), BF),
+            pltpu.VMEM((deep - 1, rows, cols), BF),
+            dma(m, wide, deep),
+            dma(m, wide, deep),
+            dma(m, deep),
+            dma(m, deep),
+        ],
+        values,
+    )
 
 
 def dot(a, b, ca, cb):
@@ -98,8 +370,7 @@
     )
     packed = padded(packed, (row_pad, col_pad))
     packed = jnp.concatenate((packed, padded(vectors[None], (16, col_pad))), axis=0)
-    whole = gather_dp(packed)
-    both = gather_seq(jnp.concatenate((tokens, cotangent), axis=1))
+    whole, both = gather_start(packed, jnp.concatenate((tokens, cotangent), axis=1))
     tokens_all = both[:, :, :D].reshape(group, D)
     upstream_all = both[:, :, D:].reshape(group, D)
 
@@ -240,6 +511,8 @@
 
 
 def solution(mesh):
+    global IDS
+    IDS = itertools.count()
     return jax.shard_map(
         body,
         mesh=mesh,

time: 730 us -> 701 us (0.960)
  Pallas kernels: 0 us -> 454 us
  waiting for transfers between devices: 424 us -> 0 us
  starting transfers between devices: 18.9 us -> 0 us
  matrix products: 54.5 us -> 37 us
  other arithmetic: 39.9 us -> 24 us
  between operations: 15.4 us -> 2.1 us
    pallas_call x0 -> x15, Pallas kernels: none -> 454 us  [run_kernel(): pl.pallas_call(kernel, out_shape=out_shapes, in_specs=[pl.BlockSpec(memor...]
    reduce_scatter x6 -> x0, waiting for transfers between devices: 211 us -> none  [the longest x1 137 us: sum_dp(): lax.psum_scatter(values, 'dp', scatter_dimension=0, tiled=False).astype(F32)]
    all_gather x6 -> x0, waiting for transfers between devices: 154 us -> none  [the longest x1 118 us: gather_dp(): return lax.all_gather(values, 'dp', axis=0, tiled=False)]
    all_to_all x4 -> x0, waiting for transfers between devices: 58.5 us -> none  [swap_seq(): lax.all_to_all(values, 'seq', split_axis=0, concat_axis=0, tiled=True)]
    dot_general x12, matrix products: 40.7 us -> 23.1 us  [dot(): lax.dot_general(a, b, (((ca,), (cb,)), ((), ())), preferred_element_type=...]
    all_to_all x4 -> x0, starting transfers between devices: 17.3 us -> none  [swap_seq(): lax.all_to_all(values, 'seq', split_axis=0, concat_axis=0, tiled=True)]
    unnamed x93 -> x107, local copies, waits for them, and re-layouts: 4.92 us -> 19.7 us
    pallas_call x0 -> x2, local copies, waits for them, and re-layouts: none -> 8.47 us  [run_kernel(): pl.pallas_call(kernel, out_shape=out_shapes, in_specs=[pl.BlockSpec(memor...]
  transfers between devices with their start and end apart: 16 -> 0, of which waited for: 11 -> 0; matrix products, arithmetic and copies ran while one was open for 23% -> 0% of each run, Pallas kernels for 0% -> 0%
where the time goes in v2:
time: 701 us; the launch traced here: 689 us
  Pallas kernels  454 us (65%)
  local copies, waits for them, and re-layouts  172 us (25%)
  matrix products  37 us (5%)
  other arithmetic  24 us (3%)
    pallas_call x15, Pallas kernels, run_kernel(): pl.pallas_call(kernel, out_shape=out_shapes, in_specs=[pl.BlockSpec(memor...  454 us
    dot_general x12, matrix products, dot(): lax.dot_general(a, b, (((ca,), (cb,)), ((), ())), preferred_element_type=...  23.1 us
    unnamed x107, local copies, waits for them, and re-layouts  19.7 us

profile of v2, /device:TPU:0, one launch (start us, length us, event | category | flops | bytes accessed | tf_op | source)
XLA Modules:
  0.0 689.1 jit_solution(12952589383463660018)
XLA Ops:
  2.4 1.7 fusion.22
  9.3 107.6 %shard_map.138 = (bf16[8,288,1664]{2,1,0:T(8,128)(2,1)}, bf16[4,128,2176]{2,1,0:T(8,128)(2,1)S(1)}) custom-call(bf16[288,1664]{1,0:T(8,128)(2,1)S(1)} %fusion.23.src, bf16[128,2176]{1,0:T(8,128)(2,1)S(1)} %pad_maximum_fusion.2.act), custom_call_target="tpu_custom_call" | custom-call | tf_op jit(solution)/shard_map/pallas_call | solution.py:66
  117.6 2.0 slice_bitcast_fusion.1
  122.5 1.8 slice.141
  124.3 4.3 slice.127
  128.7 4.4 copy.99
  133.0 2.0 copy.100
  135.0 1.9 pad.42
  136.9 7.1 %copy.142 = bf16[272,3,4,320]{3,2,0,1:T(4,128)(2,1)} copy(bf16[272,3,4,320]{0,3,2,1:T(8,128)(2,1)} %bitcast.188) | data formatting | bytes 4177920 | tf_op jit(solution)/shard_map/reshape | solution.py:388
  144.0 7.1 %copy.102 = bf16[4,272,3,320]{1,3,2,0:T(8,128)(2,1)} copy(bf16[4,272,3,320]{3,0,1,2:T(4,128)(2,1)} %bitcast.194) | data formatting | bytes 4177920 | tf_op jit(solution)/shard_map/transpose | solution.py:388
  151.1 4.4 copy.103.src
  157.2 27.4 %shard_map.140 = bf16[4,272,960]{2,1,0:T(8,128)(2,1)S(1)} custom-call(bf16[4,272,960]{2,1,0:T(8,128)(2,1)S(1)} %copy-done), custom_call_target="tpu_custom_call" | custom-call | tf_op jit(solution)/shard_map/pallas_call | solution.py:66
  186.0 6.8 slice_bitcast_fusion
  192.8 5.7 copy.96
  199.2 3.9 copy.106
  203.1 6.5 reshape_reshape.3
  209.6 2.0 copy.146
  211.6 30.1 %shard_map.143 = bf16[4,272,1088]{2,1,0:T(8,128)(2,1)S(1)} custom-call(bf16[4,272,1088]{2,1,0:T(8,128)(2,1)S(1)} %bitcast.165), custom_call_target="tpu_custom_call" | custom-call | tf_op jit(solution)/shard_map/pallas_call | solution.py:66
  243.2 19.3 %shard_map.139 = bf16[4,288,1088]{2,1,0:T(8,128)(2,1)S(1)} custom-call(bf16[288,1088]{1,0:T(8,128)(2,1)S(1)} %fusion.29.src), custom_call_target="tpu_custom_call" | custom-call | tf_op jit(solution)/shard_map/pallas_call | solution.py:66
  266.7 2.5 add_convert_fusion.1
  269.3 3.5 copy.108
  272.8 3.0 copy.109
  275.7 6.3 reshape.324
  282.0 4.4 fusion.61
  286.4 3.2 fusion.16
  293.9 15.8 %shard_map.141 = bf16[4,128,1088]{2,1,0:T(8,128)(2,1)S(1)} custom-call(bf16[4,128,1088]{2,1,0:T(8,128)(2,1)S(1)} %bitcast.167), custom_call_target="tpu_custom_call" | custom-call | tf_op jit(solution)/shard_map/pallas_call | solution.py:66
  311.2 9.6 %shard_map.142 = bf16[4,128,1088]{2,1,0:T(8,128)(2,1)S(1)} custom-call(bf16[128,1088]{1,0:T(8,128)(2,1)S(1)} %add_convert_fusion.3.src), custom_call_target="tpu_custom_call" | custom-call | tf_op jit(solution)/shard_map/pallas_call | solution.py:66
  320.8 1.9 multiply_convert_fusion.1
  323.2 3.0 fusion.62
  327.8 2.6 convolution_convert_fusion.3
  332.4 15.8 %shard_map.145 = bf16[4,128,1088]{2,1,0:T(8,128)(2,1)S(1)} custom-call(bf16[4,128,1088]{2,1,0:T(8,128)(2,1)S(1)} %bitcast.168), custom_call_target="tpu_custom_call" | custom-call | tf_op jit(solution)/shard_map/pallas_call | solution.py:66
  350.7 15.8 %shard_map.144 = bf16[4,128,1088]{2,1,0:T(8,128)(2,1)S(1)} custom-call(bf16[4,128,1088]{2,1,0:T(8,128)(2,1)S(1)} %bitcast.169), custom_call_target="tpu_custom_call" | custom-call | tf_op jit(solution)/shard_map/pallas_call | solution.py:66
  368.3 3.1 convolution_convert_fusion
  371.4 4.1 copy.125
  376.4 4.1 reshape.343
  380.5 4.1 copy.126
  384.6 4.9 copy.128
  389.5 10.9 %shard_map.146 = bf16[4,128,1088]{2,1,0:T(8,128)(2,1)S(1)} custom-call(bf16[128,1088]{1,0:T(8,128)(2,1)S(1)} %convert_element_type.149.src), custom_call_target="tpu_custom_call" | custom-call | tf_op jit(solution)/shard_map/pallas_call | solution.py:66
  404.0 3.5 multiply_convert_fusion
  409.0 1.9 fusion.21
  410.9 2.6 fusion.59
  413.8 2.3 convolution_convert_fusion.5
  417.6 2.4 copy.118
  421.6 27.1 %shard_map.149 = bf16[4,272,960]{2,1,0:T(8,128)(2,1)S(1)} custom-call(bf16[4,272,960]{2,1,0:T(8,128)(2,1)S(1)} %bitcast.166), custom_call_target="tpu_custom_call" | custom-call | tf_op jit(solution)/shard_map/pallas_call | solution.py:66
  448.7 1.7 copy.117
  450.4 15.8 %shard_map.147 = bf16[4,128,1088]{2,1,0:T(8,128)(2,1)S(1)} custom-call(bf16[4,128,1088]{2,1,0:T(8,128)(2,1)S(1)} %bitcast.170), custom_call_target="tpu_custom_call" | custom-call | tf_op jit(solution)/shard_map/pallas_call | solution.py:66
  467.7 2.2 fusion.33
  469.8 2.1 copy.135
  472.1 4.5 shard_map.151
  476.7 2.8 copy.119
  479.5 6.3 copy.120
  485.8 3.0 reshape.338
  488.8 2.9 slice.167
  491.7 2.9 copy.121
  494.6 1.7 copy.122
  496.4 4.5 copy.127
  500.8 1.7 convolution_convert_fusion.1
  502.6 30.4 %shard_map.148 = bf16[4,272,1088]{2,1,0:T(8,128)(2,1)S(1)} custom-call(bf16[4,272,1088]{2,1,0:T(8,128)(2,1)S(1)} %bitcast.174), custom_call_target="tpu_custom_call" | custom-call | tf_op jit(solution)/shard_map/pallas_call | solution.py:66
  533.7 1.8 pad_maximum_fusion
  535.5 19.8 %shard_map.150 = bf16[4,320,1088]{2,1,0:T(8,128)(2,1)S(1)} custom-call(bf16[320,1088]{1,0:T(8,128)(2,1)S(1)} %copy-done.2), custom_call_target="tpu_custom_call" | custom-call | tf_op jit(solution)/shard_map/pallas_call | solution.py:66
  556.6 2.4 copy.124
  559.0 13.2 %concatenate.38 = bf16[8,272,1632]{2,1,0:T(8,128)(2,1)} concatenate(bf16[8,272,544]{2,1,0:T(8,128)(2,1)} %bitcast.189, bf16[8,272,408]{2,1,0:T(8,128)(2,1)} %copy.127, bf16[8,272,136]{2,1,0:T(8,128)(2,1)} %bitcast.197, bf16[8,272,544]{2,1,0:T(8,128)(2,1)S(1)} %copy-done.14), dimensions={2} | concatenate | bytes 14204928 | tf_op jit(solution)/shard_map/concatenate | solution.py:473
  572.2 6.6 fusion.3.src
  578.8 104.2 %shard_map.152 = f32[288,1664]{1,0:T(8,128)S(1)} custom-call(bf16[8,288,1664]{2,1,0:T(8,128)(2,1)} %fusion.3.src), custom_call_target="tpu_custom_call" | custom-call | tf_op jit(solution)/shard_map/pallas_call | solution.py:66
  (192 shorter events, 52.1 us)
Async XLA Ops:
  0.6 7.0 %copy-start.34 = (bf16[1088,136]{0,1:T(8,128)(2,1)S(1)}, bf16[1088,136]{0,1:T(8,128)(2,1)}, u32[]{:S(2)}) copy-start(bf16[1088,136]{0,1:T(8,128)(2,1)} %param.13) | copy-start | bytes 887812
  4.1 4.3 copy-start.33
  6.4 2.8 copy-start.15
  6.5 303.4 %copy-start.36 = (f32[128]{0:T(128)}, f32[128]{0:T(128)S(1)}, u32[]{:S(2)}) copy-start(f32[128]{0:T(128)S(1)} %broadcast_multiply_fusion.2) | copy-start | bytes 1540
  7.7 1.5 copy-start.25
  155.5 1.6 copy-start
  157.2 35.6 %slice-start = ((s8[7667712]{0:T(1024)(128)(4,1)}), s8[4194304]{0:T(1024)(128)(4,1)S(1)}, s32[]{:S(2)}) async-start(s8[7667712]{0:T(1024)(128)(4,1)} %bitcast.179), calls=%async_computation | async-start | bytes 8388608
  184.6 1.4 copy-start.5
  185.9 6.8 slice-start.1
  241.7 1.5 copy-start.3
  264.7 2.1 copy-start.6
  275.7 6.3 copy-start.32
  275.7 6.3 copy-start.35
  289.6 1.6 copy-start.10
  289.6 2.8 copy-start.12
  290.2 1.0 copy-start.23
  293.9 16.0 %copy-start.16 = (bf16[128,1088]{1,0:T(8,128)(2,1)S(1)}, bf16[128,1088]{1,0:T(8,128)(2,1)}, u32[]{:S(2)}) copy-start(bf16[128,1088]{1,0:T(8,128)(2,1)} %copy-done.15) | copy-start | bytes 835588
  310.0 10.8 %copy-start.4 = (bf16[4,272,1088]{2,1,0:T(8,128)(2,1)S(1)}, bf16[4,272,1088]{2,1,0:T(8,128)(2,1)}, u32[]{:S(2)}) copy-start(bf16[4,272,1088]{2,1,0:T(8,128)(2,1)} %copy-done.3) | copy-start | bytes 7102468
  311.0 11.7 %copy-start.38 = (f32[128]{0:T(128)}, f32[128]{0:T(128)S(1)}, u32[]{:S(2)}) copy-start(f32[128]{0:T(128)S(1)} %add_rsqrt_fusion.2) | copy-start | bytes 1540
  320.8 1.9 copy-start.8
  320.8 2.1 copy-start.27
  320.8 2.4 copy-start.29
  322.7 3.5 copy-start.44
  326.2 1.6 copy-start.46
  332.4 16.3 %copy-start.39 = (f32[128]{0:T(128)S(1)}, f32[128]{0:T(128)}, u32[]{:S(2)}) copy-start(f32[128]{0:T(128)} %copy-done.38) | copy-start | bytes 1540
  350.7 16.1 %copy-start.26 = (bf16[128,1088]{1,0:T(8,128)(2,1)S(1)}, bf16[128,1088]{1,0:T(8,128)(2,1)}, u32[]{:S(2)}) copy-start(bf16[128,1088]{1,0:T(8,128)(2,1)} %copy-done.25) | copy-start | bytes 835588
  350.7 16.1 %copy-start.40 = (f32[128]{0:T(128)S(1)}, f32[128]{0:T(128)}, u32[]{:S(2)}) copy-start(f32[128]{0:T(128)} %copy-done.38) | copy-start | bytes 1540
  350.7 16.1 %copy-start.42 = (f32[128]{0:T(128)S(1)}, f32[128]{0:T(128)}, u32[]{:S(2)}) copy-start(f32[128]{0:T(128)} %broadcast_multiply_fusion.4) | copy-start | bytes 1540
  350.7 16.1 %copy-start.43 = (f32[128]{0:T(128)S(1)}, f32[128]{0:T(128)}, u32[]{:S(2)}) copy-start(f32[128]{0:T(128)} %broadcast_multiply_fusion.5) | copy-start | bytes 1540
  366.5 1.3 copy-start.30
  366.6 1.7 copy-start.45
  367.8 8.6 %copy-start.20 = (f32[128,1088]{1,0:T(8,128)}, f32[128,1088]{1,0:T(8,128)S(1)}, u32[]{:S(2)}) copy-start(f32[128,1088]{1,0:T(8,128)S(1)} %get-tuple-element.43) | copy-start | bytes 1671172
  371.4 4.1 copy-start.28
  384.6 15.8 %copy-start.13 = (bf16[4,272,1088]{2,1,0:T(8,128)(2,1)S(1)}, bf16[4,272,1088]{2,1,0:T(8,128)(2,1)}, u32[]{:S(2)}) copy-start(bf16[4,272,1088]{2,1,0:T(8,128)(2,1)} %slice.133) | copy-start | bytes 7102468
  400.4 1.0 copy-start.24
  400.4 2.4 copy-start.11
  407.5 1.5 copy-start.19
  410.9 2.9 copy-start.7
  413.8 2.3 copy-start.31
  420.0 1.6 copy-start.1
  450.4 16.3 %copy-start.17 = (bf16[128,1088]{1,0:T(8,128)(2,1)S(1)}, bf16[128,1088]{1,0:T(8,128)(2,1)}, u32[]{:S(2)}) copy-start(bf16[128,1088]{1,0:T(8,128)(2,1)} %copy-done.15) | copy-start | bytes 835588
  450.4 16.3 %copy-start.37 = (f32[128]{0:T(128)S(1)}, f32[128]{0:T(128)}, u32[]{:S(2)}) copy-start(f32[128]{0:T(128)} %copy-done.36) | copy-start | bytes 1540
  450.4 16.3 %copy-start.41 = (f32[128]{0:T(128)S(1)}, f32[128]{0:T(128)}, u32[]{:S(2)}) copy-start(f32[128]{0:T(128)} %add_rsqrt_fusion.1) | copy-start | bytes 1540
  466.2 1.4 copy-start.18
  466.3 1.4 copy-start.21
  466.7 0.8 copy-start.22
  496.4 4.5 copy-start.9
  496.4 4.5 copy-start.47
  533.7 1.8 copy-start.2
  555.3 3.7 copy-start.14
